TPU v7x, 128 devices: a whole 4x4x4 slice. The times are simulated.
128 devices in a mesh: wide: 32 (over x_lo, z, y), narrow: 4 (over x_hi, core).
Axes of the slice: x: 4 (x_hi: 2, x_lo: 2; x = x_hi * 2 + x_lo), y: 4, z: 4, core: 2. Of those that a mesh axis runs over, the one named last changes fastest.
Arguments:
- activations: bfloat16 [512, 8192], P(('wide', 'narrow')), may hold values from -6 to 6
- cotangent: bfloat16 [512, 8192], P('wide', 'narrow'), may hold values from -6 to 6
- gate_proj: bfloat16 [8192, 26624], P('narrow', 'wide'), may hold values from -0.0625 to 0.0625
- up_proj: bfloat16 [8192, 26624], P('narrow', 'wide'), may hold values from -0.0625 to 0.0625
- down_proj: bfloat16 [26624, 8192], P('wide', 'narrow'), may hold values from -0.0390625 to 0.0390625
Outputs:
- block_output: bfloat16 [512, 8192], P('wide', 'narrow')
- input_gradient: bfloat16 [512, 8192], P(('wide', 'narrow'))
- gate_gradient: bfloat16 [8192, 26624], P('narrow', 'wide')
- up_gradient: bfloat16 [8192, 26624], P('narrow', 'wide')
- down_gradient: bfloat16 [26624, 8192], P('wide', 'narrow')
All inputs are finite; a program needn't handle non-finite values.
Results may differ from a plain program's by a relative error of at most 0.005.
Values may be sent and summed in bfloat16 or wider, within the bound.
A program may use at most 128 MiB of HBM per device.

v0:
```python
import jax
import jax.numpy as jnp
from jax import lax
from jax.sharding import PartitionSpec as P


def silu_parts(gate):
    sigma = jax.nn.sigmoid(gate)
    return (gate * sigma, sigma * (1.0 + gate * (1.0 - sigma)))


def contract_rows(left, right):
    return lax.dot_general(
        left, right, (((0,), (0,)), ((), ())), preferred_element_type=jnp.float32
    )


def contract_cols(left, right):
    return lax.dot_general(
        left, right, (((1,), (1,)), ((), ())), preferred_element_type=jnp.float32
    )


def local(activations, cotangent, gate_proj, up_proj, down_proj):
    whole_rows = lax.all_gather(activations, ("wide", "narrow"), axis=0, tiled=True)
    tile_width = whole_rows.shape[1] // lax.axis_size("narrow")
    features = lax.dynamic_slice_in_dim(
        whole_rows, lax.axis_index("narrow") * tile_width, tile_width, 1
    )
    gate_part = jnp.dot(features, gate_proj, preferred_element_type=jnp.float32)
    up_part = jnp.dot(features, up_proj, preferred_element_type=jnp.float32)
    gate, up = lax.psum((gate_part, up_part), "narrow")
    active, slope = silu_parts(gate)
    hidden = (active * up).astype(jnp.bfloat16)
    block_output = lax.psum_scatter(
        jnp.dot(hidden, down_proj, preferred_element_type=jnp.float32),
        "wide",
        scatter_dimension=0,
        tiled=True,
    ).astype(jnp.bfloat16)
    upstream = lax.all_gather(cotangent, "wide", axis=0, tiled=True)
    down_gradient = contract_rows(hidden, upstream).astype(jnp.bfloat16)
    back_part = contract_cols(upstream, down_proj)
    back = lax.psum(back_part, "narrow")
    gate_delta = (back * up * slope).astype(jnp.bfloat16)
    up_delta = (back * active).astype(jnp.bfloat16)
    gate_gradient = contract_rows(features, gate_delta).astype(jnp.bfloat16)
    up_gradient = contract_rows(features, up_delta).astype(jnp.bfloat16)
    grad_tile = lax.psum_scatter(
        contract_cols(gate_delta, gate_proj) + contract_cols(up_delta, up_proj),
        "wide",
        scatter_dimension=0,
        tiled=True,
    ).astype(jnp.bfloat16)
    input_gradient = lax.all_to_all(grad_tile, "narrow", split_axis=0, concat_axis=1, tiled=True)
    return (block_output, input_gradient, gate_gradient, up_gradient, down_gradient)


def solution(mesh):
    placed = (
        P(("wide", "narrow"), None),
        P("wide", "narrow"),
        P("narrow", "wide"),
        P("narrow", "wide"),
        P("wide", "narrow"),
    )
    return jax.shard_map(
        local,
        mesh=mesh,
        in_specs=placed,
        out_specs=(
            P("wide", "narrow"),
            P(("wide", "narrow"), None),
            P("narrow", "wide"),
            P("narrow", "wide"),
            P("wide", "narrow"),
        ),
        check_vma=False,
    )
```

profile of v0, /device:TPU:0, one launch (start us, length us, event | category | flops | bytes accessed | tf_op | source)
XLA Modules:
  0.0 856.5 jit_solution(7337272134079506673)
XLA Ops:
  7.2 0.7 all-gather.4.cloned.1.call-update
  8.0 0.7 all-gather.6.cloned.1.call-update
  8.7 156.8 %all-gather.4.cloned.1.call-done = bf16[512,2048]{1,0:T(8,128)(2,1)} async-done(((bf16[16,2048]{1,0:T(8,128)(2,1)}), bf16[512,2048]{1,0:T(8,128)(2,1)}) %all-gather.4.cloned.1.call-update) | async-done | bytes 2097168 | tf_op jit(solution)/shard_map/all_gather | solution.py:41
  165.5 5.7 fusion.12
  171.2 199.3 %all-gather.6.cloned.1.call-done = bf16[128,4,8192]{2,1,0:T(4,128)(2,1)} async-done(((bf16[1,4,8192]{2,1,0:T(4,128)(2,1)}), bf16[128,4,8192]{2,1,0:T(4,128)(2,1)}) %all-gather.6.cloned.1.call-update) | async-done | bytes 8388624 | tf_op jit(solution)/shard_map/all_gather | solution.py:25
  370.5 12.5 %reshape.14 = bf16[512,8192]{1,0:T(8,128)(2,1)} reshape(bf16[128,4,8192]{2,1,0:T(4,128)(2,1)} %all-gather.6.cloned.1.call-done) | data formatting | bytes 16777216
  383.0 5.7 fusion.3
  388.8 4.7 fusion.5
  393.6 106.6 %all-reduce.3.cloned.1.call-done = (f32[512,832]{0,1:T(8,128)}, f32[512,832]{0,1:T(8,128)}, f32[512,832]{0,1:T(8,128)}) async-done(((f32[512,832]{0,1:T(8,128)}, f32[512,832]{0,1:T(8,128)}, f32[512,832]{0,1:T(8,128)}), (f32[512,832]{0,1:T(8,128)}, f32[512,832]{0,1:T(8,128)}, f32[512,832]{0,1:T(8,128)})) %all-reduce.3.cloned.1.call-update) | async-done | bytes 5111824 | tf_op jit(solution)/shard_map/psum | solution.py:32
  500.2 4.5 multiply_convert_fusion
  504.7 2.4 fusion.13
  507.3 4.5 convolution_add_fusion
  511.8 0.2 reduce-scatter.3.cloned.1.call-start
  512.0 6.6 fusion.11
  518.6 5.8 convolution_convert_fusion
  524.4 3.7 convolution_convert_fusion.2
  528.1 151.7 %reduce-scatter.5.cloned.1.call-done = f32[16,2048]{1,0:T(8,128)} async-done(((f32[512,2048]{1,0:T(8,128)}), f32[16,2048]{1,0:T(8,128)}) %reduce-scatter.5.cloned.1.call-update) | async-done | bytes 131088 | tf_op jit(solution)/shard_map/reduce_scatter | solution.py:49
  679.8 0.9 convert_element_type.28
  680.7 0.7 all_to_all.14
  681.4 4.7 all-to-all-start
  686.1 5.6 convolution_convert_fusion.1
  691.7 156.1 %reduce-scatter.3.cloned.1.call-done = f32[16,2048]{1,0:T(8,128)} async-done(((f32[512,2048]{1,0:T(8,128)}), f32[16,2048]{1,0:T(8,128)}) %reduce-scatter.3.cloned.1.call-update) | async-done | bytes 131088 | tf_op jit(solution)/shard_map/reduce_scatter | solution.py:35
  847.8 1.5 convert_element_type.25
  849.3 0.6 copy.16
  (20 shorter events, 0.3 us)
Async XLA Ops:
  7.2 381.6 %copy-start = (bf16[2048,832]{0,1:T(8,128)(2,1)S(1)}, bf16[2048,832]{0,1:T(8,128)(2,1)}, u32[]{:S(2)}) copy-start(bf16[2048,832]{0,1:T(8,128)(2,1)} %param.7) | copy-start | bytes 10223620
  7.2 158.3 %all-gather.4.cloned.1.call-start = ((), (), s32[]{:S(2)}) async-start(), calls=%async_computation.4 | async-start | bytes 2162688 | tf_op jit(solution)/shard_map/all_gather | solution.py:41
  7.9 362.6 %all-gather.6.cloned.1.call-start = ((), (), s32[]{:S(2)}) async-start(), calls=%async_computation.6 | async-start | bytes 8454144 | tf_op jit(solution)/shard_map/all_gather | solution.py:25
  8.7 491.5 %all-reduce.3.cloned.1.call-start = ((), (), s32[]{:S(2)}) async-start(), calls=%async_computation.7 | async-start | bytes 10223616 | tf_op jit(solution)/shard_map/psum | solution.py:32
  393.6 286.2 %reduce-scatter.5.cloned.1.call-start = ((), (), s32[]{:S(2)}) async-start(), calls=%async_computation.5 | async-start | bytes 4325376 | tf_op jit(solution)/shard_map/reduce_scatter | solution.py:49
  504.7 2.5 copy-start.1
  504.7 2.5 copy-start.4
  504.7 2.6 copy-start.3
  511.8 336.0 %reduce-scatter.3.cloned.1.call-start = ((), (), s32[]{:S(2)}) async-start(), calls=%async_computation.3 | async-start | bytes 4325376 | tf_op jit(solution)/shard_map/reduce_scatter | solution.py:35
  518.6 5.8 copy-start.2
  518.6 5.8 copy-start.5
  681.4 168.0 %all-to-all-start = ((bf16[4,4,2048]{2,1,0:T(4,128)(2,1)}), bf16[4,4,2048]{2,1,0:T(4,128)(2,1)S(1)}, u32[]{:S(2)}, u32[]{:S(2)}) async-start(bf16[4,4,2048]{2,1,0:T(4,128)(2,1)} %all_to_all.14), calls=%async_computation.2 | async-start | bytes 131072 | tf_op jit(solution)/shard_map/all_to_all | solution.py:55
Sparse Core Ops, SparseCore 0:
  9.7 155.7 all-gather.3
  167.2 203.2 all-gather.5
  393.7 106.4 all-reduce.2
  511.9 167.8 reduce-scatter.4
  682.0 165.7 reduce-scatter.2
where the time goes:
time: 857 us
  waiting for transfers between devices  772 us (90%)
  matrix products  44.8 us (5%)
  local copies, waits for them, and re-layouts  14 us (2%)
  between operations  13.8 us (2%)
    all_gather x1, waiting for transfers between devices, local(): lax.all_gather(activations, ('wide', 'narrow'), axis=0, tiled=True)  199 us
    all_gather x1, waiting for transfers between devices, local(): upstream = lax.all_gather(cotangent, 'wide', axis=0, tiled=True)  157 us
    reduce_scatter x1, waiting for transfers between devices, local(): lax.psum_scatter(jnp.dot(hidden, down_proj, preferred_element_type=jnp.fl...  156 us
    reduce_scatter x1, waiting for transfers between devices, local(): lax.psum_scatter(contract_cols(gate_delta, gate_proj) + contract_cols(up_...  152 us
    psum x1, waiting for transfers between devices, local(): gate, up = lax.psum((gate_part, up_part), 'narrow')  107 us
  transfers between devices with their start and end apart: 6, of which 5 were waited for; matrix products, arithmetic and copies ran while one was open for 3% of the time, Pallas kernels for 0%

commit v1 on v0

v1 whole, which is shorter than its diff:
```python
import jax
import jax.numpy as jnp
from jax import lax
from jax.experimental import pallas as pl
from jax.experimental.pallas import tpu as pltpu
from jax.sharding import PartitionSpec as P

MESH = pl.DeviceIdType.MESH
BF = jnp.bfloat16
F32 = jnp.float32

XL, Z, Y = 2, 4, 4
ROWS = 16
TILE = 2048
HALF = TILE // 2
FFL = 832
QUART = 64
STEP = 512


def dot(a, b):
    return lax.dot_general(a, b, (((1,), (0,)), ((), ())), preferred_element_type=F32)


def dot_t(a, b):
    return lax.dot_general(a, b, (((1,), (1,)), ((), ())), preferred_element_type=F32)


def kernel(
    act, cot, wg_hbm, wu_hbm, wd_hbm,
    out_ref, ig_ref, f_hbm, c_hbm, h_hbm, gd_hbm, ud_hbm,
    wg, wu, wd, feat, cota, a_send, a_recv, a_f32,
    g_send, g_own, g_recv, x_send, x_recv, hd,
    part, r1_send, r1_recv, s1, r2_send, r2_recv, xo_send, xo_recv, t_f32, o_f32, n_send, n_recv,
    w_sem, o_sem, a_ss, a_rs, cx_ss, cx_rs, p1_ss, p1_rs, p2_ss, p2_rs,
    g_ss, g_rs, x_ss, x_rs, h_ss, h_rs, r1_ss, r1_rs, r2_ss, r2_rs, xo_ss, xo_rs, n_ss, n_rs,
):
    w = lax.axis_index("wide")
    n = lax.axis_index("narrow")
    y = lax.rem(w, Y)
    z = lax.rem(w // Y, Z)
    xl = w // (Y * Z)
    xh = n // 2
    core = lax.rem(n, 2)
    quarter = core * 2 + xh
    far_quarter = core * 2 + (1 - xh)

    def wide_id(a, b, c):
        return (a * Z + b) * Y + c

    def y_dev(d):
        return (wide_id(xl, z, lax.rem(y + d, Y)), n)

    def z_dev(d):
        return (wide_id(xl, lax.rem(z + d, Z), y), n)

    def line_dev(dx, dn):
        return (wide_id(lax.rem(xl + dx, XL), z, y), lax.rem(n + dn, 4))

    sibling = (w, xh * 2 + (1 - core))
    across = (w, (1 - xh) * 2 + core)
    peer = (wide_id(1 - xl, z, y), n)
    line = [(dx, dn) for dx in range(XL) for dn in range(4) if (dx, dn) != (0, 0)]

    sends = []

    def remote(src, dst, ss, rs, dev):
        return pltpu.make_async_remote_copy(
            src_ref=src, dst_ref=dst, send_sem=ss, recv_sem=rs, device_id=dev, device_id_type=MESH
        )

    def send(src, dst, ss, rs, dev):
        copy = remote(src, dst, ss, rs, dev)
        copy.start()
        sends.append(copy)

    def landed(dst, ss, rs, dev):
        remote(dst, dst, ss, rs, dev).wait_recv()

    loads = [
        pltpu.make_async_copy(src, dst, w_sem.at[i])
        for i, (src, dst) in enumerate(((wg_hbm, wg), (wu_hbm, wu), (wd_hbm, wd)))
    ]
    for load in loads:
        load.start()

    barrier = pltpu.get_barrier_semaphore()
    friends = [y_dev(d) for d in (1, 2, 3)] + [z_dev(d) for d in (1, 2, 3)] + [line_dev(*k) for k in line]
    for dev in friends:
        pl.semaphore_signal(barrier, inc=1, device_id=dev, device_id_type=MESH)

    rows4 = act[...].astype(F32)
    for m in range(4):
        for k in range(4):
            at = m * TILE + k * STEP
            t_f32[m, pl.ds(4 * k, 4), :] = rows4[:, at : at + STEP]
    for m in range(4):
        a_send[m] = t_f32[m].astype(BF)
    cota[xl, z, y] = cot[...]

    pl.semaphore_wait(barrier, len(friends))

    here = xl * 4 + n
    for i, (dx, dn) in enumerate(line):
        m = lax.rem(n + dn, 4)
        send(a_send.at[m], a_recv.at[here], a_ss.at[i], a_rs.at[i], line_dev(dx, dn))
    send(cota.at[xl, z, y], cota.at[xl, z, y], cx_ss, cx_rs, peer)
    a_recv[here] = a_send[n]
    for i, (dx, dn) in enumerate(line):
        src = lax.rem(xl + dx, XL) * 4 + lax.rem(n + 4 - dn, 4)
        landed(a_recv.at[src], a_ss.at[i], a_rs.at[i], line_dev(dx, dn))
    for s in range(8):
        t_f32[s] = a_recv[s].astype(F32)
        for k in range(4):
            a_f32[s // 4, pl.ds(4 * (s % 4), 4), pl.ds(k * STEP, STEP)] = t_f32[s, pl.ds(4 * k, 4), :]
    for c in range(XL):
        feat[c, z, y] = a_f32[c].astype(BF)

    bufs = (feat, cota)
    cols = (pl.ds(0, HALF), pl.ds(HALF, HALF))

    def gather1(b, c):
        block = [bufs[b].at[c, z, y, :, cols[h]] for h in (0, 1)]
        for d in (1, 2, 3):
            send(block[0], block[0], p1_ss.at[b, c, 0, d - 1], p1_rs.at[b, c, 0, d - 1], z_dev(d))
            send(block[1], block[1], p1_ss.at[b, c, 1, d - 1], p1_rs.at[b, c, 1, d - 1], y_dev(d))

    def gather1_wait(b, c):
        for d in (1, 2, 3):
            landed(bufs[b].at[c, lax.rem(z + 4 - d, Z), y, :, cols[0]], p1_ss.at[b, c, 0, d - 1], p1_rs.at[b, c, 0, d - 1], z_dev(d))
            landed(bufs[b].at[c, z, lax.rem(y + 4 - d, Y), :, cols[1]], p1_ss.at[b, c, 1, d - 1], p1_rs.at[b, c, 1, d - 1], y_dev(d))

    low, high = pl.ds(0, 2), pl.ds(2, 2)

    def ring_block(b, c, h, back, part_of):
        if h == 0:
            return bufs[b].at[c, part_of, lax.rem(y + 4 - back, Y), :, cols[0]]
        return bufs[b].at[c, lax.rem(z + 4 - back, Z), part_of, :, cols[1]]

    def ring_dev(h, d):
        return y_dev(d) if h == 0 else z_dev(d)

    def gather2(b, c):
        for i, (d, part_of) in enumerate(((1, low), (3, high), (1, high), (3, low))):
            for h in (0, 1):
                block = ring_block(b, c, h, 0, part_of)
                send(block, block, p2_ss.at[b, c, h, i], p2_rs.at[b, c, h, i], ring_dev(h, d))

    def gather2_pass_on(b, c):
        for i, (d, part_of) in enumerate(((1, low), (3, high))):
            for h in (0, 1):
                block = ring_block(b, c, h, d, part_of)
                landed(block, p2_ss.at[b, c, h, i], p2_rs.at[b, c, h, i], ring_dev(h, d))
                send(block, block, p2_ss.at[b, c, h, 4 + i], p2_rs.at[b, c, h, 4 + i], ring_dev(h, d))

    def gather2_wait(b, c):
        for i, (d, back, part_of) in ((2, (1, 1, high)), (3, (3, 3, low)), (4, (1, 2, low)), (5, (3, 2, high))):
            for h in (0, 1):
                landed(ring_block(b, c, h, back, part_of), p2_ss.at[b, c, h, i], p2_rs.at[b, c, h, i], ring_dev(h, d))

    def partial(c, half, ks, into):
        for k in ks:
            if k == 2:
                v = dot_t(cota[c, pl.ds(2 * half, 2)].reshape(2 * QUART, TILE), wd[...])
            else:
                v = dot_t(feat[c, pl.ds(2 * half, 2)].reshape(2 * QUART, TILE), (wg, wu)[k][...])
            into[c, k] = v.reshape(2, QUART, FFL)

    groups = ((0, 2), (2, 1))

    def sum_send(c, g):
        first, count = groups[g]
        partial(c, 1 - core, range(first, first + count), g_send)
        ks = pl.ds(first, count)
        send(g_send.at[c, ks], g_recv.at[c, ks], g_ss.at[c, g], g_rs.at[c, g], sibling)

    def sum_own(c, g):
        first, count = groups[g]
        partial(c, core, range(first, first + count), g_own)

    def sum_across(c, g):
        first, count = groups[g]
        ks = pl.ds(first, count)
        landed(g_recv.at[c, ks], g_ss.at[c, g], g_rs.at[c, g], sibling)
        for k in range(first, first + count):
            x_send[c, k] = (g_own[c, k, 1 - xh] + g_recv[c, k, 1 - xh]).astype(BF)
        send(x_send.at[c, ks], x_recv.at[c, ks], x_ss.at[c, g], x_rs.at[c, g], across)

    def total(c, k):
        return g_own[c, k, xh] + g_recv[c, k, xh] + x_recv[c, k].astype(F32)

    def spread(c, g):
        ks = pl.ds(*((0, 1), (1, 2))[g])
        block = hd.at[ks, c, quarter]
        send(block, block, h_ss.at[c, g, 0], h_rs.at[c, g, 0], across)
        send(block, block, h_ss.at[c, g, 1], h_rs.at[c, g, 1], sibling)

    def spread_pass_on(c, g):
        ks = pl.ds(*((0, 1), (1, 2))[g])
        block = hd.at[ks, c, far_quarter]
        landed(block, h_ss.at[c, g, 0], h_rs.at[c, g, 0], across)
        send(block, block, h_ss.at[c, g, 2], h_rs.at[c, g, 2], sibling)

    def spread_wait(c, g):
        ks = pl.ds(*((0, 1), (1, 2))[g])
        other = (1 - core) * 2
        landed(hd.at[ks, c, other + xh], h_ss.at[c, g, 1], h_rs.at[c, g, 1], sibling)
        landed(hd.at[ks, c, other + 1 - xh], h_ss.at[c, g, 2], h_rs.at[c, g, 2], sibling)

    def hidden(c):
        landed(x_recv.at[c, pl.ds(0, 2)], x_ss.at[c, 0], x_rs.at[c, 0], across)
        gate, up = total(c, 0), total(c, 1)
        hd[0, c, quarter] = (gate * lax.logistic(gate) * up).astype(BF)
        spread(c, 0)

    def deltas(c):
        landed(x_recv.at[c, pl.ds(2, 1)], x_ss.at[c, 1], x_rs.at[c, 1], across)
        gate, up, back = total(c, 0), total(c, 1), total(c, 2)
        sigma = lax.logistic(gate)
        hd[1, c, quarter] = (back * up * (sigma * (1.0 + gate * (1.0 - sigma)))).astype(BF)
        hd[2, c, quarter] = (back * (gate * sigma)).astype(BF)
        spread(c, 1)

    def product(k, c):
        def columns(j, carry):
            at = pl.ds(pl.multiple_of(j * STEP, STEP), STEP)
            if k == 0:
                v = dot(hd[0, c].reshape(4 * QUART, FFL), wd[:, at])
            else:
                v = dot(hd[1, c].reshape(4 * QUART, FFL), wg[:, at])
                v += dot(hd[2, c].reshape(4 * QUART, FFL), wu[:, at])
            v = v.reshape(Z, Y, ROWS, STEP)
            part[k, c, :, :, :, at] = v
            r1_send[k, c, :, :, :, at] = v.astype(BF)
            return carry

        lax.fori_loop(0, TILE // STEP, columns, 0)
        for d in (1, 2, 3):
            send(r1_send.at[k, c, :, lax.rem(y + d, Y), :, cols[0]], r1_recv.at[k, c, 0, d - 1], r1_ss.at[k, c, 0, d - 1], r1_rs.at[k, c, 0, d - 1], y_dev(d))
            send(r1_send.at[k, c, lax.rem(z + d, Z), :, :, cols[1]], r1_recv.at[k, c, 1, d - 1], r1_ss.at[k, c, 1, d - 1], r1_rs.at[k, c, 1, d - 1], z_dev(d))

    def scatter2(k, c):
        for h in (0, 1):
            for d in (1, 2, 3):
                landed(r1_recv.at[k, c, h, d - 1], r1_ss.at[k, c, h, d - 1], r1_rs.at[k, c, h, d - 1], ring_dev(h, d))
            own = part[k, c, :, y, :, cols[0]] if h == 0 else part[k, c, z, :, :, cols[1]]
            for d in (1, 2, 3):
                own += r1_recv[k, c, h, d - 1].astype(F32)
            s1[k, c, h] = own
            r2_send[k, c, h] = own.astype(BF)
            for d in (1, 2, 3):
                to = lax.rem((z if h == 0 else y) + d, 4)
                send(r2_send.at[k, c, h, to], r2_recv.at[k, c, h, d - 1], r2_ss.at[k, c, h, d - 1], r2_rs.at[k, c, h, d - 1], ring_dev(1 - h, d))

    def scattered(k, c):
        for h in (0, 1):
            for d in (1, 2, 3):
                landed(r2_recv.at[k, c, h, d - 1], r2_ss.at[k, c, h, d - 1], r2_rs.at[k, c, h, d - 1], ring_dev(1 - h, d))
            own = s1[k, c, h, z if h == 0 else y]
            for d in (1, 2, 3):
                own += r2_recv[k, c, h, d - 1].astype(F32)
            xo_send[k, c, :, cols[h]] = own

    def output_peer(c):
        copy = remote(xo_send.at[0, c], xo_recv, xo_ss, xo_rs, peer)
        pl.when(xl != c)(copy.start)

    def owners(c):
        for m in range(4):
            for k in range(4):
                t_f32[m, pl.ds(4 * k, 4), :] = xo_send[1, c, pl.ds(4 * m, 4), pl.ds(k * STEP, STEP)]
        for m in range(4):
            n_send[c, m] = t_f32[m].astype(BF)
        dx = lax.rem(c + 2 - xl, XL)
        for dn in range(4):
            m = lax.rem(n + dn, 4)
            copy = remote(n_send.at[c, m], n_recv.at[here], n_ss.at[c, dn], n_rs.at[dx, dn], (wide_id(c, z, y), m))
            if dn == 0:
                pl.when(xl != c)(copy.start)
            else:
                copy.start()
                sends.append(copy)

    for b, c in ((0, 0), (0, 1)):
        gather1(b, c)
    landed(cota.at[1 - xl, z, y], cx_ss, cx_rs, peer)
    gather1(1, 0)
    gather1_wait(0, 0)
    gather2(0, 0)
    gather1(1, 1)
    gather1_wait(1, 0)
    gather2_pass_on(0, 0)
    gather2(1, 0)
    for load in loads:
        load.wait()
    gather2_wait(0, 0)
    sum_send(0, 0)
    gather2_pass_on(1, 0)
    gather1_wait(0, 1)
    gather2(0, 1)
    sum_own(0, 0)
    sum_across(0, 0)
    gather2_wait(1, 0)
    gather2_pass_on(0, 1)
    gather1_wait(1, 1)
    gather2(1, 1)
    sum_send(0, 1)
    sum_own(0, 1)
    sum_across(0, 1)
    gather2_wait(0, 1)
    gather2_pass_on(1, 1)
    sum_send(1, 0)
    sum_own(1, 0)
    hidden(0)
    sum_across(1, 0)
    deltas(0)
    gather2_wait(1, 1)
    stores = [
        pltpu.make_async_copy(feat, f_hbm, o_sem.at[0]),
        pltpu.make_async_copy(cota, c_hbm, o_sem.at[1]),
    ]
    for store in stores:
        store.start()
    sum_send(1, 1)
    sum_own(1, 1)
    sum_across(1, 1)
    spread_pass_on(0, 0)
    spread_wait(0, 0)
    product(0, 0)
    spread_pass_on(0, 1)
    hidden(1)
    spread_wait(0, 1)
    product(1, 0)
    deltas(1)
    scatter2(0, 0)
    spread_pass_on(1, 0)
    spread_wait(1, 0)
    product(0, 1)
    scatter2(1, 0)
    spread_pass_on(1, 1)
    spread_wait(1, 1)
    product(1, 1)
    for k in range(3):
        stores.append(pltpu.make_async_copy(hd.at[k], (h_hbm, gd_hbm, ud_hbm)[k], o_sem.at[2 + k]))
        stores[-1].start()
    scattered(0, 0)
    output_peer(0)
    scatter2(0, 1)
    scattered(1, 0)
    owners(0)
    scatter2(1, 1)
    scattered(0, 1)
    output_peer(1)
    scattered(1, 1)
    owners(1)
    landed(xo_recv, xo_ss, xo_rs, peer)
    out_ref[...] = (xo_send[0, xl] + xo_recv[...]).astype(BF)
    n_recv[here] = n_send[xl, n]
    for dx, dn in line:
        src = lax.rem(xl + dx, XL) * 4 + lax.rem(n + 4 - dn, 4)
        landed(n_recv.at[src], n_ss.at[0, 0], n_rs.at[dx, dn], line_dev(dx, dn))
    for m in range(4):
        t_f32[m] = n_recv[m].astype(F32) + n_recv[4 + m].astype(F32)
        for k in range(4):
            at = m * TILE + k * STEP
            o_f32[:, pl.ds(at, STEP)] = t_f32[m, pl.ds(4 * k, 4), :]
    ig_ref[...] = o_f32[...].astype(BF)

    for copy in sends:
        copy.wait_send()
    remote(xo_send.at[0, 1 - xl], xo_recv, xo_ss, xo_rs, peer).wait_send()
    remote(n_send.at[1 - xl, n], n_recv.at[here], n_ss.at[1 - xl, 0], n_rs.at[1, 0], peer).wait_send()
    for store in stores:
        store.wait()


def forward_backward(act, cot, gate_proj, up_proj, down_proj):
    any_space = pl.BlockSpec(memory_space=pl.ANY)
    vmem = pl.BlockSpec(memory_space=pltpu.VMEM)
    sem = pltpu.SemaphoreType.DMA
    rows = (XL, Z, Y, ROWS, TILE)
    units = (XL, 4, QUART, FFL)
    like = jax.ShapeDtypeStruct
    flops = 2 * 6 * XL * Z * Y * ROWS * TILE * FFL
    return pl.pallas_call(
        kernel,
        name="ffn",
        out_shape=[
            like((ROWS, TILE), BF), like((4, 4 * TILE), BF),
            like(rows, BF), like(rows, BF), like(units, BF), like(units, BF), like(units, BF),
        ],
        in_specs=[vmem, vmem, any_space, any_space, any_space],
        out_specs=[vmem, vmem] + [any_space] * 5,
        scratch_shapes=[
            pltpu.VMEM((FFL, TILE), BF), pltpu.VMEM((FFL, TILE), BF), pltpu.VMEM((FFL, TILE), BF),
            pltpu.VMEM(rows, BF), pltpu.VMEM(rows, BF),
            pltpu.VMEM((4, 16, STEP), BF), pltpu.VMEM((8, 16, STEP), BF), pltpu.VMEM((XL, ROWS, TILE), F32),
            pltpu.VMEM((XL, 3, 2, QUART, FFL), F32), pltpu.VMEM((XL, 3, 2, QUART, FFL), F32), pltpu.VMEM((XL, 3, 2, QUART, FFL), F32),
            pltpu.VMEM((XL, 3, QUART, FFL), BF), pltpu.VMEM((XL, 3, QUART, FFL), BF),
            pltpu.VMEM((3, XL, 4, QUART, FFL), BF),
            pltpu.VMEM((2,) + rows, F32), pltpu.VMEM((2,) + rows, BF),
            pltpu.VMEM((2, XL, 2, 3, 4, ROWS, HALF), BF),
            pltpu.VMEM((2, XL, 2, 4, ROWS, HALF), F32), pltpu.VMEM((2, XL, 2, 4, ROWS, HALF), BF),
            pltpu.VMEM((2, XL, 2, 3, ROWS, HALF), BF),
            pltpu.VMEM((2, XL, ROWS, TILE), F32), pltpu.VMEM((ROWS, TILE), F32),
            pltpu.VMEM((8, 16, STEP), F32), pltpu.VMEM((4, 4 * TILE), F32),
            pltpu.VMEM((XL, 4, 16, STEP), BF), pltpu.VMEM((8, 16, STEP), BF),
            sem((3,)), sem((5,)), sem((7,)), sem((7,)), sem, sem,
            sem((2, XL, 2, 3)), sem((2, XL, 2, 3)), sem((2, XL, 2, 6)), sem((2, XL, 2, 6)),
            sem((XL, 2)), sem((XL, 2)), sem((XL, 2)), sem((XL, 2)), sem((XL, 2, 3)), sem((XL, 2, 3)),
            sem((2, XL, 2, 3)), sem((2, XL, 2, 3)), sem((2, XL, 2, 3)), sem((2, XL, 2, 3)),
            sem, sem, sem((XL, 4)), sem((XL, 4)),
        ],
        compiler_params=pltpu.CompilerParams(
            collective_id=0, has_side_effects=True, vmem_limit_bytes=62 * 1024 * 1024
        ),
        cost_estimate=pl.CostEstimate(flops=flops, bytes_accessed=20 * 1024 * 1024, transcendentals=0),
    )(act, cot, gate_proj, up_proj, down_proj)


def contract_rows(left, right):
    return lax.dot_general(left, right, (((0,), (0,)), ((), ())), preferred_element_type=F32).astype(BF)


def local(activations, cotangent, gate_proj, up_proj, down_proj):
    block_output, input_gradient, features, upstream, hid, gate_delta, up_delta = forward_backward(
        activations, cotangent, gate_proj.T, up_proj.T, down_proj
    )
    tokens = XL * Z * Y * ROWS
    features, upstream = features.reshape(tokens, TILE), upstream.reshape(tokens, TILE)
    hid, gate_delta, up_delta = (a.reshape(tokens, FFL) for a in (hid, gate_delta, up_delta))
    return (
        block_output,
        input_gradient,
        contract_rows(gate_delta, features).T,
        contract_rows(up_delta, features).T,
        contract_rows(hid, upstream),
    )


def solution(mesh):
    placed = (
        P(("wide", "narrow"), None),
        P("wide", "narrow"),
        P("narrow", "wide"),
        P("narrow", "wide"),
        P("wide", "narrow"),
    )
    return jax.shard_map(
        local,
        mesh=mesh,
        in_specs=placed,
        out_specs=(
            P("wide", "narrow"),
            P(("wide", "narrow"), None),
            P("narrow", "wide"),
            P("narrow", "wide"),
            P("wide", "narrow"),
        ),
        check_vma=False,
    )
```

time: 857 us -> 109 us (0.13)
  waiting for transfers between devices: 772 us -> 0 us
  Pallas kernels: 0 us -> 92.5 us
  matrix products: 44.8 us -> 13.2 us
  between operations: 13.8 us -> 0.68 us
  local copies, waits for them, and re-layouts: 14 us -> 1.28 us
    all_gather x2 -> x0, waiting for transfers between devices: 356 us -> none  [the longest x1 199 us: local(): lax.all_gather(activations, ('wide', 'narrow'), axis=0, tiled=True)]
    reduce_scatter x2 -> x0, waiting for transfers between devices: 308 us -> none  [the longest x1 156 us: local(): lax.psum_scatter(jnp.dot(hidden, down_proj, preferred_element_type=jnp.fl...]
    psum x1 -> x0, waiting for transfers between devices: 107 us -> none  [local(): gate, up = lax.psum((gate_part, up_part), 'narrow')]
    pallas_call x0 -> x1, Pallas kernels: none -> 92.5 us  [forward_backward(): pl.pallas_call(kernel, name='ffn', out_shape=[like((ROWS, TILE), BF), lik...]
    dot_general x6 -> x0, matrix products: 29.7 us -> none  [the longest x3 12.6 us: contract_cols(): lax.dot_general(left, right, (((1,), (1,)), ((), ())), preferred_element_...]
    unnamed x14, local copies, waits for them, and re-layouts: 13.3 us -> 1.28 us
  transfers between devices with their start and end apart: 6 -> 0, of which waited for: 5 -> 0; matrix products, arithmetic and copies ran while one was open for 3% -> 0% of each run, Pallas kernels for 0% -> 0%
where the time goes in v1:
time: 109 us; the launch traced here: 108 us
  Pallas kernels  92.5 us (85%)
  matrix products  13.2 us (12%)
  local copies, waits for them, and re-layouts  1.28 us (1%)
    pallas_call x1, Pallas kernels, forward_backward(): pl.pallas_call(kernel, name='ffn', out_shape=[like((ROWS, TILE), BF), lik...  92.5 us
    dot_general x3, matrix products, contract_rows(): lax.dot_general(left, right, (((0,), (0,)), ((), ())), preferred_element_...  13.2 us

profile of v1, /device:TPU:0, one launch (start us, length us, event | category | flops | bytes accessed | tf_op | source)
XLA Modules:
  0.0 107.6 jit_solution(8418636896386347644)
XLA Ops:
  0.6 92.5 %ffn.1 = (bf16[16,2048]{1,0:T(8,128)(2,1)}, bf16[4,8192]{1,0:T(4,128)(2,1)}, bf16[2,4,4,16,2048]{4,3,2,1,0:T(8,128)(2,1)}, bf16[2,4,4,16,2048]{4,3,2,1,0:T(8,128...) custom-call(bf16[4,8192]{1,0:T(4,128)(2,1)} %act.1, ...), custom_call_target="tpu_custom_call" | custom-call | flops 10468982784 | bytes 20971520 | tf_op jit(solution)/shard_map/ffn/pallas_call | solution.py:385
  93.1 0.0 copy-start.3
  93.1 0.0 copy-start.5
  93.1 5.7 %convolution_convert_fusion.1 = bf16[2048,832]{0,1:T(8,128)(2,1)} fusion(bf16[512,2048]{1,0:T(8,128)(2,1)} %bitcast.16, bf16[512,832]{1,0:T(8,128)(2,1)} %bitcast.20), kind=kOutput, calls=%fused_computation.1 | convolution fusion | flops 1746534400 | bytes 6356992 | tf_op jit(solution)/shard_map/dot_general | solution.py:422
  98.8 0.0 copy-done.3
  98.8 0.0 copy-done.5
  98.8 0.0 copy-start.2
  98.8 0.0 copy-start.4
  98.8 3.8 %convolution_convert_fusion.2 = bf16[2048,832]{0,1:T(8,128)(2,1)} fusion(bf16[512,2048]{1,0:T(8,128)(2,1)S(1)} %bitcast.17, bf16[512,832]{1,0:T(8,128)(2,1)S(1)} %bitcast.19), kind=kOutput, calls=%fused_computation.2 | convolution fusion | flops 1746534400 | bytes 6356992 | tf_op jit(solution)/shard_map/dot_general | solution.py:422
  102.6 0.0 copy-done.2
  102.6 0.0 copy-done.4
  102.6 0.0 copy-start.1
  102.6 0.0 copy-start
  102.6 3.7 %convolution_convert_fusion = bf16[832,2048]{1,0:T(8,128)(2,1)} fusion(bf16[512,832]{1,0:T(8,128)(2,1)S(1)} %bitcast.18, bf16[512,2048]{1,0:T(8,128)(2,1)S(1)} %bitcast.15), kind=kOutput, calls=%fused_computation | convolution fusion | flops 1746534400 | bytes 6356992 | tf_op jit(solution)/shard_map/dot_general | solution.py:422
  106.3 0.0 copy-done.1
  106.3 0.6 copy.12
  107.0 0.0 copy-done
  107.0 0.6 copy.13
Async XLA Ops:
  93.1 5.7 %copy-start.3 = (bf16[2,4,4,16,2048]{4,3,2,1,0:T(8,128)(2,1)S(1)}, bf16[2,4,4,16,2048]{4,3,2,1,0:T(8,128)(2,1)}, u32[]{:S(2)}) copy-start(bf16[2,4,4,16,2048]{4,3,2,1,0:T(8,128)(2,1)} %get-tuple-element.14) | copy-start | bytes 6291460
  93.1 5.7 %copy-start.5 = (bf16[2,4,64,832]{3,2,1,0:T(8,128)(2,1)S(1)}, bf16[2,4,64,832]{3,2,1,0:T(8,128)(2,1)}, u32[]{:S(2)}) copy-start(bf16[2,4,64,832]{3,2,1,0:T(8,128)(2,1)} %get-tuple-element.15) | copy-start | bytes 2555908
  98.8 3.8 %copy-start.2 = (bf16[2,4,4,16,2048]{4,3,2,1,0:T(8,128)(2,1)S(1)}, bf16[2,4,4,16,2048]{4,3,2,1,0:T(8,128)(2,1)}, u32[]{:S(2)}) copy-start(bf16[2,4,4,16,2048]{4,3,2,1,0:T(8,128)(2,1)} %get-tuple-element.18) | copy-start | bytes 6291460
  98.8 3.8 %copy-start.4 = (bf16[2,4,64,832]{3,2,1,0:T(8,128)(2,1)S(1)}, bf16[2,4,64,832]{3,2,1,0:T(8,128)(2,1)}, u32[]{:S(2)}) copy-start(bf16[2,4,64,832]{3,2,1,0:T(8,128)(2,1)} %get-tuple-element.17) | copy-start | bytes 2555908
  102.6 3.7 %copy-start.1 = (bf16[16,2048]{1,0:T(8,128)(2,1)S(1)}, bf16[16,2048]{1,0:T(8,128)(2,1)}, u32[]{:S(2)}) copy-start(bf16[16,2048]{1,0:T(8,128)(2,1)} %get-tuple-element.24) | copy-start | bytes 196612
  102.6 4.4 %copy-start = (bf16[4,8192]{1,0:T(4,128)(2,1)S(1)}, bf16[4,8192]{1,0:T(4,128)(2,1)}, u32[]{:S(2)}) copy-start(bf16[4,8192]{1,0:T(4,128)(2,1)} %get-tuple-element.25) | copy-start | bytes 196612

commit v2 on v1

v2 whole, which is shorter than its diff:
```python
import jax
import jax.numpy as jnp
from jax import lax
from jax.experimental import pallas as pl
from jax.experimental.pallas import tpu as pltpu
from jax.sharding import PartitionSpec as P

MESH = pl.DeviceIdType.MESH
BF = jnp.bfloat16
F32 = jnp.float32

XL, Z, Y = 2, 4, 4
ROWS = 16
TILE = 2048
HALF = TILE // 2
FFL = 832
CHUNK = Z * Y * ROWS
PART = FFL // 2
STEP = 512


def dot(a, b):
    return lax.dot_general(a, b, (((1,), (0,)), ((), ())), preferred_element_type=F32)


def dot_t(a, b):
    return lax.dot_general(a, b, (((1,), (1,)), ((), ())), preferred_element_type=F32)


def kernel(
    act, cot, wg_hbm, wu_hbm, wd_hbm,
    out_ref, ig_ref, down_hbm, gate_hbm, up_hbm,
    wg, wu, wd, feat, cota, a_send, a_recv, a_f32,
    g_send, g_own, g_recv, x_send, x_recv, hd, ht,
    part, r1_send, r1_recv, s1, r2_send, r2_recv, xo_send, xo_recv, t_f32, o_f32, n_send, n_recv, grad,
    w_sem, o_sem, a_ss, a_rs, cx_ss, cx_rs, p1_ss, p1_rs, p2_ss, p2_rs,
    g_ss, g_rs, x_ss, x_rs, h_ss, h_rs, r1_ss, r1_rs, r2_ss, r2_rs, xo_ss, xo_rs, n_ss, n_rs,
):
    w = lax.axis_index("wide")
    n = lax.axis_index("narrow")
    y = lax.rem(w, Y)
    z = lax.rem(w // Y, Z)
    xl = w // (Y * Z)
    xh = n // 2
    core = lax.rem(n, 2)

    def wide_id(a, b, c):
        return (a * Z + b) * Y + c

    def y_dev(d):
        return (wide_id(xl, z, lax.rem(y + d, Y)), n)

    def z_dev(d):
        return (wide_id(xl, lax.rem(z + d, Z), y), n)

    def line_dev(dx, dn):
        return (wide_id(lax.rem(xl + dx, XL), z, y), lax.rem(n + dn, 4))

    sibling = (w, xh * 2 + (1 - core))
    across = (w, (1 - xh) * 2 + core)
    peer = (wide_id(1 - xl, z, y), n)
    line = [(dx, dn) for dx in range(XL) for dn in range(4) if (dx, dn) != (0, 0)]

    sends = []

    def remote(src, dst, ss, rs, dev):
        return pltpu.make_async_remote_copy(
            src_ref=src, dst_ref=dst, send_sem=ss, recv_sem=rs, device_id=dev, device_id_type=MESH
        )

    def send(src, dst, ss, rs, dev):
        copy = remote(src, dst, ss, rs, dev)
        copy.start()
        sends.append(copy)

    def landed(dst, ss, rs, dev):
        remote(dst, dst, ss, rs, dev).wait_recv()

    loads = [
        pltpu.make_async_copy(src, dst, w_sem.at[i])
        for i, (src, dst) in enumerate(((wg_hbm, wg), (wu_hbm, wu), (wd_hbm, wd)))
    ]
    for load in loads:
        load.start()

    barrier = pltpu.get_barrier_semaphore()
    friends = [y_dev(d) for d in (1, 2, 3)] + [z_dev(d) for d in (1, 2, 3)] + [line_dev(*k) for k in line]
    for dev in friends:
        pl.semaphore_signal(barrier, inc=1, device_id=dev, device_id_type=MESH)

    rows4 = act[...].astype(F32)
    for m in range(4):
        for k in range(4):
            at = m * TILE + k * STEP
            t_f32[m, pl.ds(4 * k, 4), :] = rows4[:, at : at + STEP]
    for m in range(4):
        a_send[m] = t_f32[m].astype(BF)
    cota[0, z, y] = cot[...]

    pl.semaphore_wait(barrier, len(friends))

    def exchange(dx):
        for i, (ex, dn) in enumerate(line):
            if ex == dx:
                send(a_send.at[lax.rem(n + dn, 4)], a_recv.at[4 * dx + n], a_ss.at[i], a_rs.at[i], line_dev(dx, dn))

    def assemble(dx):
        for i, (ex, dn) in enumerate(line):
            if ex == dx:
                landed(a_recv.at[4 * dx + lax.rem(n + 4 - dn, 4)], a_ss.at[i], a_rs.at[i], line_dev(dx, dn))
        for m in range(4):
            t_f32[m] = a_recv[4 * dx + m].astype(F32)
            for k in range(4):
                a_f32[dx, pl.ds(4 * m, 4), pl.ds(k * STEP, STEP)] = t_f32[m, pl.ds(4 * k, 4), :]
        feat[dx, z, y] = a_f32[dx].astype(BF)

    bufs = (feat, cota)
    cols = (pl.ds(0, HALF), pl.ds(HALF, HALF))

    def gather1(b, c):
        block = [bufs[b].at[c, z, y, :, cols[h]] for h in (0, 1)]
        for d in (1, 2, 3):
            send(block[0], block[0], p1_ss.at[b, c, 0, d - 1], p1_rs.at[b, c, 0, d - 1], z_dev(d))
            send(block[1], block[1], p1_ss.at[b, c, 1, d - 1], p1_rs.at[b, c, 1, d - 1], y_dev(d))

    def gather1_wait(b, c):
        for d in (1, 2, 3):
            landed(bufs[b].at[c, lax.rem(z + 4 - d, Z), y, :, cols[0]], p1_ss.at[b, c, 0, d - 1], p1_rs.at[b, c, 0, d - 1], z_dev(d))
            landed(bufs[b].at[c, z, lax.rem(y + 4 - d, Y), :, cols[1]], p1_ss.at[b, c, 1, d - 1], p1_rs.at[b, c, 1, d - 1], y_dev(d))

    low, high = pl.ds(0, 2), pl.ds(2, 2)

    def ring_block(b, c, h, back, part_of):
        if h == 0:
            return bufs[b].at[c, part_of, lax.rem(y + 4 - back, Y), :, cols[0]]
        return bufs[b].at[c, lax.rem(z + 4 - back, Z), part_of, :, cols[1]]

    def ring_dev(h, d):
        return y_dev(d) if h == 0 else z_dev(d)

    def gather2(b, c):
        for i, (d, part_of) in enumerate(((1, low), (3, high), (1, high), (3, low))):
            for h in (0, 1):
                block = ring_block(b, c, h, 0, part_of)
                send(block, block, p2_ss.at[b, c, h, i], p2_rs.at[b, c, h, i], ring_dev(h, d))

    def gather2_pass_on(b, c):
        for i, (d, part_of) in enumerate(((1, low), (3, high))):
            for h in (0, 1):
                block = ring_block(b, c, h, d, part_of)
                landed(block, p2_ss.at[b, c, h, i], p2_rs.at[b, c, h, i], ring_dev(h, d))
                send(block, block, p2_ss.at[b, c, h, 4 + i], p2_rs.at[b, c, h, 4 + i], ring_dev(h, d))

    def gather2_wait(b, c):
        for i, (d, back, part_of) in ((2, (1, 1, high)), (3, (3, 3, low)), (4, (1, 2, low)), (5, (3, 2, high))):
            for h in (0, 1):
                landed(ring_block(b, c, h, back, part_of), p2_ss.at[b, c, h, i], p2_rs.at[b, c, h, i], ring_dev(h, d))

    def partial(c, core_of, k, into):
        rows = pl.ds(pl.multiple_of(PART * core_of, PART), PART)
        into[c, k] = dot_t((wg, wu, wd)[k][rows, :], (feat, feat, cota)[k][c].reshape(CHUNK, TILE))

    def sum_send(c, k):
        partial(c, 1 - core, k, g_send)
        send(g_send.at[c, k], g_recv.at[c, k], g_ss.at[c, k], g_rs.at[c, k], sibling)

    def sum_own(c, k):
        partial(c, core, k, g_own)

    def sum_across(c, k):
        landed(g_recv.at[c, k], g_ss.at[c, k], g_rs.at[c, k], sibling)
        v = g_own[c, k] + g_recv[c, k]
        g_own[c, k] = v
        x_send[c, k] = v.astype(BF)
        send(x_send.at[c, k], x_recv.at[c, k], x_ss.at[c, k], x_rs.at[c, k], across)

    def arrived(c, k):
        landed(x_recv.at[c, k], x_ss.at[c, k], x_rs.at[c, k], across)
        return g_own[c, k] + x_recv[c, k].astype(F32)

    tokens = (pl.ds(0, CHUNK), pl.ds(CHUNK, CHUNK))

    def share(c, g):
        block = hd.at[pl.ds(*((0, 1), (1, 2))[g]), core, :, tokens[c]]
        send(block, block, h_ss.at[c, g], h_rs.at[c, g], sibling)

    def share_wait(c, g):
        block = hd.at[pl.ds(*((0, 1), (1, 2))[g]), 1 - core, :, tokens[c]]
        landed(block, h_ss.at[c, g], h_rs.at[c, g], sibling)

    def hidden(c):
        gate, up = arrived(c, 0), arrived(c, 1)
        g_own[c, 0] = gate
        g_own[c, 1] = up
        hd[0, core, :, tokens[c]] = (gate * lax.logistic(gate) * up).astype(BF)
        share(c, 0)

    def deltas(c):
        gate, up, back = g_own[c, 0], g_own[c, 1], arrived(c, 2)
        sigma = lax.logistic(gate)
        hd[1, core, :, tokens[c]] = (back * up * (sigma * (1.0 + gate * (1.0 - sigma)))).astype(BF)
        hd[2, core, :, tokens[c]] = (back * (gate * sigma)).astype(BF)
        share(c, 1)

    def product(k, c):
        for i in ((0,), (1, 2))[k]:
            ht[i] = hd[i, :, :, tokens[c]].reshape(FFL, CHUNK).T

        for h in (0, 1):
            if k == 0:
                v = dot(ht[0], wd[:, cols[h]])
            else:
                v = dot(ht[1], wg[:, cols[h]]) + dot(ht[2], wu[:, cols[h]])
            v = v.reshape(Z, Y, ROWS, HALF)
            part[...] = v
            r1_send[k, c, :, :, :, cols[h]] = v.astype(BF)
            for d in (1, 2, 3):
                to = lax.rem((y, z)[h] + d, 4)
                block = r1_send.at[k, c, :, to, :, cols[0]] if h == 0 else r1_send.at[k, c, to, :, :, cols[1]]
                send(block, r1_recv.at[k, c, h, d - 1], r1_ss.at[k, c, h, d - 1], r1_rs.at[k, c, h, d - 1], ring_dev(h, d))
            s1[k, c, h] = part[:, y] if h == 0 else part[z]

    def scatter2(k, c):
        for h in (0, 1):
            for d in (1, 2, 3):
                landed(r1_recv.at[k, c, h, d - 1], r1_ss.at[k, c, h, d - 1], r1_rs.at[k, c, h, d - 1], ring_dev(h, d))
            own = s1[k, c, h]
            for d in (1, 2, 3):
                own += r1_recv[k, c, h, d - 1].astype(F32)
            s1[k, c, h] = own
            r2_send[k, c, h] = own.astype(BF)
            for d in (1, 2, 3):
                to = lax.rem((z if h == 0 else y) + d, 4)
                send(r2_send.at[k, c, h, to], r2_recv.at[k, c, h, d - 1], r2_ss.at[k, c, h, d - 1], r2_rs.at[k, c, h, d - 1], ring_dev(1 - h, d))

    def scattered(k, c):
        for h in (0, 1):
            for d in (1, 2, 3):
                landed(r2_recv.at[k, c, h, d - 1], r2_ss.at[k, c, h, d - 1], r2_rs.at[k, c, h, d - 1], ring_dev(1 - h, d))
            own = s1[k, c, h, z if h == 0 else y]
            for d in (1, 2, 3):
                own += r2_recv[k, c, h, d - 1].astype(F32)
            xo_send[k, c, :, cols[h]] = own

    def owners(c):
        for m in range(4):
            for k in range(4):
                t_f32[m, pl.ds(4 * k, 4), :] = xo_send[1, c, pl.ds(4 * m, 4), pl.ds(k * STEP, STEP)]
        for m in range(4):
            n_send[c, m] = t_f32[m].astype(BF)
        for i, (dx, dn) in enumerate(line):
            if dx == c:
                send(n_send.at[c, lax.rem(n + dn, 4)], n_recv.at[4 * c + n], n_ss.at[i], n_rs.at[i], line_dev(dx, dn))

    stores = []

    def gradient(k):
        def columns(j, carry):
            at = pl.ds(pl.multiple_of(j * STEP, STEP), STEP)
            right = (cota, feat, feat)[k][:, :, :, :, at].reshape(XL * CHUNK, STEP)
            grad[k, :, at] = dot(hd[k].reshape(FFL, XL * CHUNK), right).astype(BF)
            return carry

        lax.fori_loop(0, TILE // STEP, columns, 0)
        stores.append(pltpu.make_async_copy(grad.at[k], (down_hbm, gate_hbm, up_hbm)[k], o_sem.at[k]))
        stores[-1].start()

    exchange(0)
    gather1(1, 0)
    exchange(1)
    send(cota.at[0, z, y], cota.at[1, z, y], cx_ss, cx_rs, peer)
    a_recv[n] = a_send[n]
    assemble(0)
    gather1(0, 0)
    gather1_wait(1, 0)
    gather2(1, 0)
    gather1_wait(0, 0)
    gather2(0, 0)
    gather2_pass_on(1, 0)
    assemble(1)
    gather1(0, 1)
    landed(cota.at[1, z, y], cx_ss, cx_rs, peer)
    gather1(1, 1)
    gather2_pass_on(0, 0)
    for load in loads:
        load.wait()
    gather1_wait(0, 1)
    gather2(0, 1)
    gather2_wait(0, 0)
    sum_send(0, 0)
    sum_send(0, 1)
    sum_own(0, 0)
    gather2_wait(1, 0)
    gather2_pass_on(0, 1)
    gather1_wait(1, 1)
    gather2(1, 1)
    sum_across(0, 0)
    sum_own(0, 1)
    sum_across(0, 1)
    sum_send(0, 2)
    sum_own(0, 2)
    sum_across(0, 2)
    gather2_wait(0, 1)
    sum_send(1, 0)
    sum_send(1, 1)
    gather2_pass_on(1, 1)
    sum_own(1, 0)
    sum_across(1, 0)
    sum_own(1, 1)
    sum_across(1, 1)
    hidden(0)
    gather2_wait(1, 1)
    sum_send(1, 2)
    share_wait(0, 0)
    product(0, 0)
    sum_own(1, 2)
    sum_across(1, 2)
    deltas(0)
    share_wait(0, 1)
    product(1, 0)
    scatter2(0, 0)
    hidden(1)
    share_wait(1, 0)
    product(0, 1)
    deltas(1)
    share_wait(1, 1)
    product(1, 1)
    scatter2(1, 0)
    gradient(0)
    scattered(0, 0)
    scatter2(0, 1)
    gradient(1)
    scattered(1, 0)
    owners(0)
    gradient(2)
    scattered(0, 1)
    send(xo_send.at[0, 1], xo_recv, xo_ss, xo_rs, peer)
    scatter2(1, 1)
    scattered(1, 1)
    owners(1)
    landed(xo_recv, xo_ss, xo_rs, peer)
    out_ref[...] = (xo_send[0, 0] + xo_recv[...]).astype(BF)
    n_recv[n] = n_send[0, n]
    for i, (dx, dn) in enumerate(line):
        landed(n_recv.at[4 * dx + lax.rem(n + 4 - dn, 4)], n_ss.at[i], n_rs.at[i], line_dev(dx, dn))
    for m in range(4):
        t_f32[m] = n_recv[m].astype(F32) + n_recv[4 + m].astype(F32)
        for k in range(4):
            at = m * TILE + k * STEP
            o_f32[:, pl.ds(at, STEP)] = t_f32[m, pl.ds(4 * k, 4), :]
    ig_ref[...] = o_f32[...].astype(BF)

    for copy in sends:
        copy.wait_send()
    for store in stores:
        store.wait()


def forward_backward(act, cot, gate_proj, up_proj, down_proj):
    any_space = pl.BlockSpec(memory_space=pl.ANY)
    vmem = pl.BlockSpec(memory_space=pltpu.VMEM)
    sem = pltpu.SemaphoreType.DMA
    rows = (XL, Z, Y, ROWS, TILE)
    like = jax.ShapeDtypeStruct
    flops = 2 * 9 * XL * Z * Y * ROWS * TILE * FFL
    return pl.pallas_call(
        kernel,
        name="ffn",
        out_shape=[
            like((ROWS, TILE), BF), like((4, 4 * TILE), BF),
            like((FFL, TILE), BF), like((FFL, TILE), BF), like((FFL, TILE), BF),
        ],
        in_specs=[vmem, vmem, any_space, any_space, any_space],
        out_specs=[vmem, vmem] + [any_space] * 3,
        scratch_shapes=[
            pltpu.VMEM((FFL, TILE), BF), pltpu.VMEM((FFL, TILE), BF), pltpu.VMEM((FFL, TILE), BF),
            pltpu.VMEM(rows, BF), pltpu.VMEM(rows, BF),
            pltpu.VMEM((4, 16, STEP), BF), pltpu.VMEM((8, 16, STEP), BF), pltpu.VMEM((XL, ROWS, TILE), F32),
            pltpu.VMEM((XL, 3, PART, CHUNK), F32), pltpu.VMEM((XL, 3, PART, CHUNK), F32), pltpu.VMEM((XL, 3, PART, CHUNK), F32),
            pltpu.VMEM((XL, 3, PART, CHUNK), BF), pltpu.VMEM((XL, 3, PART, CHUNK), BF),
            pltpu.VMEM((3, 2, PART, XL * CHUNK), BF), pltpu.VMEM((3, CHUNK, FFL), BF),
            pltpu.VMEM((Z, Y, ROWS, HALF), F32), pltpu.VMEM((2,) + rows, BF),
            pltpu.VMEM((2, XL, 2, 3, 4, ROWS, HALF), BF),
            pltpu.VMEM((2, XL, 2, 4, ROWS, HALF), F32), pltpu.VMEM((2, XL, 2, 4, ROWS, HALF), BF),
            pltpu.VMEM((2, XL, 2, 3, ROWS, HALF), BF),
            pltpu.VMEM((2, XL, ROWS, TILE), F32), pltpu.VMEM((ROWS, TILE), F32),
            pltpu.VMEM((8, 16, STEP), F32), pltpu.VMEM((4, 4 * TILE), F32),
            pltpu.VMEM((XL, 4, 16, STEP), BF), pltpu.VMEM((8, 16, STEP), BF), pltpu.VMEM((3, FFL, TILE), BF),
            sem((3,)), sem((3,)), sem((7,)), sem((7,)), sem, sem,
            sem((2, XL, 2, 3)), sem((2, XL, 2, 3)), sem((2, XL, 2, 6)), sem((2, XL, 2, 6)),
            sem((XL, 3)), sem((XL, 3)), sem((XL, 3)), sem((XL, 3)), sem((XL, 2)), sem((XL, 2)),
            sem((2, XL, 2, 3)), sem((2, XL, 2, 3)), sem((2, XL, 2, 3)), sem((2, XL, 2, 3)),
            sem, sem, sem((7,)), sem((7,)),
        ],
        compiler_params=pltpu.CompilerParams(
            collective_id=0, has_side_effects=True, vmem_limit_bytes=62 * 1024 * 1024
        ),
        cost_estimate=pl.CostEstimate(flops=flops, bytes_accessed=20 * 1024 * 1024, transcendentals=0),
    )(act, cot, gate_proj, up_proj, down_proj)


SLABS = 4


def move(*refs):
    srcs, dsts, held, sem_in, sem_out = refs[:5], refs[5:10], refs[10:15], refs[15], refs[16]
    parts = []
    for src, via, dst in zip(srcs, held, dsts):
        slabs = SLABS if src.shape[0] == FFL else 1
        rows = src.shape[0] // slabs
        for i in range(slabs):
            at, j = pl.ds(i * rows, rows), len(parts)
            parts.append((
                pltpu.make_async_copy(src.at[at], via.at[at], sem_in.at[j]),
                pltpu.make_async_copy(via.at[at], dst.at[at], sem_out.at[j]),
            ))
    for load, _ in parts:
        load.start()
    for load, store in parts:
        load.wait()
        store.start()
    for _, store in parts:
        store.wait()


def local(activations, cotangent, gate_proj, up_proj, down_proj):
    results = forward_backward(activations, cotangent, gate_proj.T, up_proj.T, down_proj)
    any_space = pl.BlockSpec(memory_space=pl.ANY)
    block_output, input_gradient, down_gradient, gate_gradient, up_gradient = pl.pallas_call(
        move,
        name="move",
        out_shape=[jax.ShapeDtypeStruct(r.shape, r.dtype) for r in results],
        in_specs=[any_space] * 5,
        out_specs=[any_space] * 5,
        scratch_shapes=[pltpu.VMEM(r.shape, r.dtype) for r in results]
        + [pltpu.SemaphoreType.DMA((3 * SLABS + 2,))] * 2,
        compiler_params=pltpu.CompilerParams(vmem_limit_bytes=62 * 1024 * 1024),
    )(*results)
    return block_output, input_gradient, gate_gradient.T, up_gradient.T, down_gradient


def solution(mesh):
    placed = (
        P(("wide", "narrow"), None),
        P("wide", "narrow"),
        P("narrow", "wide"),
        P("narrow", "wide"),
        P("wide", "narrow"),
    )
    return jax.shard_map(
        local,
        mesh=mesh,
        in_specs=placed,
        out_specs=(
            P("wide", "narrow"),
            P(("wide", "narrow"), None),
            P("narrow", "wide"),
            P("narrow", "wide"),
            P("wide", "narrow"),
        ),
        check_vma=False,
    )
```

time: 109 us -> 99.5 us (0.913)
  matrix products: 13.2 us -> 0 us
  Pallas kernels: 92.5 us -> 97.5 us
  local copies, waits for them, and re-layouts: 1.28 us -> 0 us
    dot_general x3 -> x0, matrix products: 13.2 us -> none  [contract_rows(): lax.dot_general(left, right, (((0,), (0,)), ((), ())), preferred_element_...]
    pallas_call x0 -> x1, Pallas kernels: none -> 8.01 us  [local(): pl.pallas_call(move, name='move', out_shape=[jax.ShapeDtypeStruct(r.shape...]
    pallas_call x1, Pallas kernels: 92.5 us -> 89.5 us  [forward_backward(): pl.pallas_call(kernel, name='ffn', out_shape=[like((ROWS, TILE), BF), lik...]
    unnamed x14 -> x0, local copies, waits for them, and re-layouts: 1.28 us -> none
where the time goes in v2:
time: 99.5 us; the launch traced here: 98.3 us
  Pallas kernels  97.5 us (98%)
    pallas_call x1, Pallas kernels, forward_backward(): pl.pallas_call(kernel, name='ffn', out_shape=[like((ROWS, TILE), BF), lik...  89.5 us
    pallas_call x1, Pallas kernels, local(): pl.pallas_call(move, name='move', out_shape=[jax.ShapeDtypeStruct(r.shape...  8.01 us

profile of v2, /device:TPU:0, one launch (start us, length us, event | category | flops | bytes accessed | tf_op | source)
XLA Modules:
  0.0 98.3 jit_solution(6697310424513018810)
XLA Ops:
  0.6 89.5 %ffn.1 = (bf16[16,2048]{1,0:T(8,128)(2,1)}, bf16[4,8192]{1,0:T(4,128)(2,1)}, bf16[832,2048]{1,0:T(8,128)(2,1)}, bf16[832,2048]{1,0:T(8,128)(2,1)}, bf16[832,2048]{1,0:T(8,128)(2,1)}) custom-call(bf16[4,8192]{1,0:T(4,128)(2,1)} %act.1, bf16[16,2048]{1,0:T(8,128)(2,1)} %cot.1, bf16[832,2048]{1,0:T(8,128)(2,1)} %bitcast.4, bf16[832,2048]{1,0:T(8,128)(2,1)} %bitcast.5, ...), custom_call_target="tpu_custom_call" | custom-call | flops 15703474176 | bytes 20971520 | tf_op jit(solution)/shard_map/ffn/pallas_call | solution.py:366
  90.1 8.0 %move.1 = (bf16[16,2048]{1,0:T(8,128)(2,1)}, bf16[4,8192]{1,0:T(4,128)(2,1)}, bf16[832,2048]{1,0:T(8,128)(2,1)}, bf16[832,2048]{1,0:T(8,128)(2,1)}, bf16[832,2048]{1,0:T(8,128)(2,1)}) custom-call(bf16[16,2048]{1,0:T(8,128)(2,1)} %get-tuple-element.15.refs_0_, bf16[4,8192]{1,0:T(4,128)(2,1)} %get-tuple-element.16.refs_1_, ...), custom_call_target="tpu_custom_call" | custom-call | tf_op jit(solution)/shard_map/move/pallas_call | solution.py:429

commit v3 on v2

--- a/solution.py
+++ b/solution.py
@@ -15,6 +15,8 @@
 HALF = TILE // 2
 FFL = 832
 CHUNK = Z * Y * ROWS
+SUB = CHUNK // 2
+OWN = Z - 1
 PART = FFL // 2
 STEP = 512
 
@@ -95,7 +97,7 @@
             t_f32[m, pl.ds(4 * k, 4), :] = rows4[:, at : at + STEP]
     for m in range(4):
         a_send[m] = t_f32[m].astype(BF)
-    cota[0, z, y] = cot[...]
+    cota[0, OWN, y] = cot[...]
 
     pl.semaphore_wait(barrier, len(friends))
 
@@ -112,28 +114,31 @@
             t_f32[m] = a_recv[4 * dx + m].astype(F32)
             for k in range(4):
                 a_f32[dx, pl.ds(4 * m, 4), pl.ds(k * STEP, STEP)] = t_f32[m, pl.ds(4 * k, 4), :]
-        feat[dx, z, y] = a_f32[dx].astype(BF)
+        feat[dx, OWN, y] = a_f32[dx].astype(BF)
 
     bufs = (feat, cota)
     cols = (pl.ds(0, HALF), pl.ds(HALF, HALF))
 
     def gather1(b, c):
-        block = [bufs[b].at[c, z, y, :, cols[h]] for h in (0, 1)]
+        block = [bufs[b].at[c, OWN, y, :, cols[h]] for h in (0, 1)]
         for d in (1, 2, 3):
-            send(block[0], block[0], p1_ss.at[b, c, 0, d - 1], p1_rs.at[b, c, 0, d - 1], z_dev(d))
+            send(block[0], bufs[b].at[c, OWN - d, y, :, cols[0]], p1_ss.at[b, c, 0, d - 1], p1_rs.at[b, c, 0, d - 1], z_dev(d))
             send(block[1], block[1], p1_ss.at[b, c, 1, d - 1], p1_rs.at[b, c, 1, d - 1], y_dev(d))
 
     def gather1_wait(b, c):
         for d in (1, 2, 3):
-            landed(bufs[b].at[c, lax.rem(z + 4 - d, Z), y, :, cols[0]], p1_ss.at[b, c, 0, d - 1], p1_rs.at[b, c, 0, d - 1], z_dev(d))
-            landed(bufs[b].at[c, z, lax.rem(y + 4 - d, Y), :, cols[1]], p1_ss.at[b, c, 1, d - 1], p1_rs.at[b, c, 1, d - 1], y_dev(d))
+            landed(bufs[b].at[c, OWN - d, y, :, cols[0]], p1_ss.at[b, c, 0, d - 1], p1_rs.at[b, c, 0, d - 1], z_dev(d))
+            landed(bufs[b].at[c, OWN, lax.rem(y + 4 - d, Y), :, cols[1]], p1_ss.at[b, c, 1, d - 1], p1_rs.at[b, c, 1, d - 1], y_dev(d))
 
     low, high = pl.ds(0, 2), pl.ds(2, 2)
 
     def ring_block(b, c, h, back, part_of):
         if h == 0:
             return bufs[b].at[c, part_of, lax.rem(y + 4 - back, Y), :, cols[0]]
-        return bufs[b].at[c, lax.rem(z + 4 - back, Z), part_of, :, cols[1]]
+        return bufs[b].at[c, OWN - back, part_of, :, cols[1]]
+
+    def ring_block_at(b, c, h, back, part_of, d):
+        return ring_block(b, c, h, back if h == 0 else (back + d) % 4, part_of)
 
     def ring_dev(h, d):
         return y_dev(d) if h == 0 else z_dev(d)
@@ -141,15 +146,15 @@
     def gather2(b, c):
         for i, (d, part_of) in enumerate(((1, low), (3, high), (1, high), (3, low))):
             for h in (0, 1):
-                block = ring_block(b, c, h, 0, part_of)
-                send(block, block, p2_ss.at[b, c, h, i], p2_rs.at[b, c, h, i], ring_dev(h, d))
+                block, there = ring_block(b, c, h, 0, part_of), ring_block_at(b, c, h, 0, part_of, d)
+                send(block, there, p2_ss.at[b, c, h, i], p2_rs.at[b, c, h, i], ring_dev(h, d))
 
     def gather2_pass_on(b, c):
         for i, (d, part_of) in enumerate(((1, low), (3, high))):
             for h in (0, 1):
-                block = ring_block(b, c, h, d, part_of)
+                block, there = ring_block(b, c, h, d, part_of), ring_block_at(b, c, h, d, part_of, d)
                 landed(block, p2_ss.at[b, c, h, i], p2_rs.at[b, c, h, i], ring_dev(h, d))
-                send(block, block, p2_ss.at[b, c, h, 4 + i], p2_rs.at[b, c, h, 4 + i], ring_dev(h, d))
+                send(block, there, p2_ss.at[b, c, h, 4 + i], p2_rs.at[b, c, h, 4 + i], ring_dev(h, d))
 
     def gather2_wait(b, c):
         for i, (d, back, part_of) in ((2, (1, 1, high)), (3, (3, 3, low)), (4, (1, 2, low)), (5, (3, 2, high))):
@@ -167,78 +172,98 @@
     def sum_own(c, k):
         partial(c, core, k, g_own)
 
-    def sum_across(c, k):
+    subs = (pl.ds(0, SUB), pl.ds(SUB, SUB))
+
+    def sum_chip(c, k):
         landed(g_recv.at[c, k], g_ss.at[c, k], g_rs.at[c, k], sibling)
         v = g_own[c, k] + g_recv[c, k]
         g_own[c, k] = v
-        x_send[c, k] = v.astype(BF)
-        send(x_send.at[c, k], x_recv.at[c, k], x_ss.at[c, k], x_rs.at[c, k], across)
-
-    def arrived(c, k):
-        landed(x_recv.at[c, k], x_ss.at[c, k], x_rs.at[c, k], across)
-        return g_own[c, k] + x_recv[c, k].astype(F32)
-
-    tokens = (pl.ds(0, CHUNK), pl.ds(CHUNK, CHUNK))
-
-    def share(c, g):
-        block = hd.at[pl.ds(*((0, 1), (1, 2))[g]), core, :, tokens[c]]
-        send(block, block, h_ss.at[c, g], h_rs.at[c, g], sibling)
-
-    def share_wait(c, g):
-        block = hd.at[pl.ds(*((0, 1), (1, 2))[g]), 1 - core, :, tokens[c]]
-        landed(block, h_ss.at[c, g], h_rs.at[c, g], sibling)
-
-    def hidden(c):
-        gate, up = arrived(c, 0), arrived(c, 1)
-        g_own[c, 0] = gate
-        g_own[c, 1] = up
-        hd[0, core, :, tokens[c]] = (gate * lax.logistic(gate) * up).astype(BF)
-        share(c, 0)
-
-    def deltas(c):
-        gate, up, back = g_own[c, 0], g_own[c, 1], arrived(c, 2)
+        for s in (0, 1):
+            x_send[c, k, s] = v[:, s * SUB : (s + 1) * SUB].astype(BF)
+
+    def sum_across(c, k, s):
+        send(x_send.at[c, k, s], x_recv.at[c, k, s], x_ss.at[c, k, s], x_rs.at[c, k, s], across)
+
+    def arrived(c, k, s):
+        landed(x_recv.at[c, k, s], x_ss.at[c, k, s], x_rs.at[c, k, s], across)
+        return g_own[c, k, :, subs[s]] + x_recv[c, k, s].astype(F32)
+
+    def tokens(c, s):
+        return pl.ds(c * CHUNK + s * SUB, SUB)
+
+    def share(c, s, g):
+        block = hd.at[pl.ds(*((0, 1), (1, 2))[g]), core, :, tokens(c, s)]
+        send(block, block, h_ss.at[c, s, g], h_rs.at[c, s, g], sibling)
+
+    def share_wait(c, s, g):
+        block = hd.at[pl.ds(*((0, 1), (1, 2))[g]), 1 - core, :, tokens(c, s)]
+        landed(block, h_ss.at[c, s, g], h_rs.at[c, s, g], sibling)
+
+    def hidden(c, s):
+        gate, up = arrived(c, 0, s), arrived(c, 1, s)
+        g_own[c, 0, :, subs[s]] = gate
+        g_own[c, 1, :, subs[s]] = up
+        hd[0, core, :, tokens(c, s)] = (gate * lax.logistic(gate) * up).astype(BF)
+        share(c, s, 0)
+
+    def deltas(c, s):
+        gate, up, back = g_own[c, 0, :, subs[s]], g_own[c, 1, :, subs[s]], arrived(c, 2, s)
         sigma = lax.logistic(gate)
-        hd[1, core, :, tokens[c]] = (back * up * (sigma * (1.0 + gate * (1.0 - sigma)))).astype(BF)
-        hd[2, core, :, tokens[c]] = (back * (gate * sigma)).astype(BF)
-        share(c, 1)
-
-    def product(k, c):
+        hd[1, core, :, tokens(c, s)] = (back * up * (sigma * (1.0 + gate * (1.0 - sigma)))).astype(BF)
+        hd[2, core, :, tokens(c, s)] = (back * (gate * sigma)).astype(BF)
+        share(c, s, 1)
+
+    def product(k, c, s):
+        share_wait(c, s, k)
         for i in ((0,), (1, 2))[k]:
-            ht[i] = hd[i, :, :, tokens[c]].reshape(FFL, CHUNK).T
-
+            ht[i] = hd[i, :, :, tokens(c, s)].reshape(FFL, SUB).T
+        zs = pl.ds(2 * s, 2)
         for h in (0, 1):
             if k == 0:
                 v = dot(ht[0], wd[:, cols[h]])
             else:
                 v = dot(ht[1], wg[:, cols[h]]) + dot(ht[2], wu[:, cols[h]])
-            v = v.reshape(Z, Y, ROWS, HALF)
+            v = v.reshape(2, Y, ROWS, HALF)
             part[...] = v
-            r1_send[k, c, :, :, :, cols[h]] = v.astype(BF)
-            for d in (1, 2, 3):
-                to = lax.rem((y, z)[h] + d, 4)
-                block = r1_send.at[k, c, :, to, :, cols[0]] if h == 0 else r1_send.at[k, c, to, :, :, cols[1]]
-                send(block, r1_recv.at[k, c, h, d - 1], r1_ss.at[k, c, h, d - 1], r1_rs.at[k, c, h, d - 1], ring_dev(h, d))
-            s1[k, c, h] = part[:, y] if h == 0 else part[z]
-
-    def scatter2(k, c):
-        for h in (0, 1):
-            for d in (1, 2, 3):
-                landed(r1_recv.at[k, c, h, d - 1], r1_ss.at[k, c, h, d - 1], r1_rs.at[k, c, h, d - 1], ring_dev(h, d))
-            own = s1[k, c, h]
-            for d in (1, 2, 3):
-                own += r1_recv[k, c, h, d - 1].astype(F32)
-            s1[k, c, h] = own
-            r2_send[k, c, h] = own.astype(BF)
-            for d in (1, 2, 3):
-                to = lax.rem((z if h == 0 else y) + d, 4)
-                send(r2_send.at[k, c, h, to], r2_recv.at[k, c, h, d - 1], r2_ss.at[k, c, h, d - 1], r2_rs.at[k, c, h, d - 1], ring_dev(1 - h, d))
+            r1_send[k, c, zs, :, :, cols[h]] = v.astype(BF)
+            if h == 0:
+                for d in (1, 2, 3):
+                    send(r1_send.at[k, c, zs, lax.rem(y + d, Y), :, cols[0]], r1_recv.at[k, c, 0, d - 1, zs], r1_ss.at[k, c, s, d - 1], r1_rs.at[k, c, s, d - 1], y_dev(d))
+                s1[k, c, 0, zs] = part[:, y]
+            else:
+                for j in (2 * s, 2 * s + 1):
+                    if j == OWN:
+                        s1[k, c, 1] = part[1]
+                    else:
+                        send(r1_send.at[k, c, j, :, :, cols[1]], r1_recv.at[k, c, 1, j], r1_ss.at[k, c, 2, j], r1_rs.at[k, c, 2, j], z_dev(j + 1))
+
+    def scatter_z(k, c, s):
+        zs = pl.ds(2 * s, 2)
+        own = s1[k, c, 0, zs]
+        for d in (1, 2, 3):
+            landed(r1_recv.at[k, c, 0, d - 1, zs], r1_ss.at[k, c, s, d - 1], r1_rs.at[k, c, s, d - 1], y_dev(d))
+            own += r1_recv[k, c, 0, d - 1, zs].astype(F32)
+        s1[k, c, 0, zs] = own
+        r2_send[k, c, 0, zs] = own.astype(BF)
+        for j in (2 * s, 2 * s + 1):
+            if j != OWN:
+                send(r2_send.at[k, c, 0, j], r2_recv.at[k, c, 0, j], r2_ss.at[k, c, 0, j], r2_rs.at[k, c, 0, j], z_dev(j + 1))
+
+    def scatter_y(k, c):
+        own = s1[k, c, 1]
+        for j in (0, 1, 2):
+            landed(r1_recv.at[k, c, 1, j], r1_ss.at[k, c, 2, j], r1_rs.at[k, c, 2, j], z_dev(j + 1))
+            own += r1_recv[k, c, 1, j].astype(F32)
+        s1[k, c, 1] = own
+        r2_send[k, c, 1] = own.astype(BF)
+        for d in (1, 2, 3):
+            send(r2_send.at[k, c, 1, lax.rem(y + d, Y)], r2_recv.at[k, c, 1, d - 1], r2_ss.at[k, c, 1, d - 1], r2_rs.at[k, c, 1, d - 1], y_dev(d))
 
     def scattered(k, c):
         for h in (0, 1):
+            own = s1[k, c, h, OWN if h == 0 else y]
             for d in (1, 2, 3):
                 landed(r2_recv.at[k, c, h, d - 1], r2_ss.at[k, c, h, d - 1], r2_rs.at[k, c, h, d - 1], ring_dev(1 - h, d))
-            own = s1[k, c, h, z if h == 0 else y]
-            for d in (1, 2, 3):
                 own += r2_recv[k, c, h, d - 1].astype(F32)
             xo_send[k, c, :, cols[h]] = own
 
@@ -265,10 +290,15 @@
         stores.append(pltpu.make_async_copy(grad.at[k], (down_hbm, gate_hbm, up_hbm)[k], o_sem.at[k]))
         stores[-1].start()
 
+    def sent(upto):
+        for copy in sends[:upto]:
+            copy.wait_send()
+        del sends[:upto]
+
     exchange(0)
     gather1(1, 0)
     exchange(1)
-    send(cota.at[0, z, y], cota.at[1, z, y], cx_ss, cx_rs, peer)
+    send(cota.at[0, OWN, y], cota.at[1, OWN, y], cx_ss, cx_rs, peer)
     a_recv[n] = a_send[n]
     assemble(0)
     gather1(0, 0)
@@ -279,7 +309,7 @@
     gather2_pass_on(1, 0)
     assemble(1)
     gather1(0, 1)
-    landed(cota.at[1, z, y], cx_ss, cx_rs, peer)
+    landed(cota.at[1, OWN, y], cx_ss, cx_rs, peer)
     gather1(1, 1)
     gather2_pass_on(0, 0)
     for load in loads:
@@ -294,48 +324,74 @@
     gather2_pass_on(0, 1)
     gather1_wait(1, 1)
     gather2(1, 1)
-    sum_across(0, 0)
+    sum_chip(0, 0)
+    sum_across(0, 0, 0)
     sum_own(0, 1)
-    sum_across(0, 1)
+    sum_chip(0, 1)
+    sum_across(0, 1, 0)
+    sum_across(0, 0, 1)
+    sum_across(0, 1, 1)
     sum_send(0, 2)
     sum_own(0, 2)
-    sum_across(0, 2)
+    sum_chip(0, 2)
+    sum_across(0, 2, 0)
+    sum_across(0, 2, 1)
     gather2_wait(0, 1)
     sum_send(1, 0)
     sum_send(1, 1)
     gather2_pass_on(1, 1)
+    hidden(0, 0)
     sum_own(1, 0)
-    sum_across(1, 0)
+    product(0, 0, 0)
+    sum_chip(1, 0)
+    sum_across(1, 0, 0)
     sum_own(1, 1)
-    sum_across(1, 1)
-    hidden(0)
+    sum_chip(1, 1)
+    sum_across(1, 1, 0)
+    sum_across(1, 0, 1)
+    sum_across(1, 1, 1)
+    hidden(0, 1)
     gather2_wait(1, 1)
     sum_send(1, 2)
-    share_wait(0, 0)
-    product(0, 0)
+    product(0, 0, 1)
+    deltas(0, 0)
     sum_own(1, 2)
-    sum_across(1, 2)
-    deltas(0)
-    share_wait(0, 1)
-    product(1, 0)
-    scatter2(0, 0)
-    hidden(1)
-    share_wait(1, 0)
-    product(0, 1)
-    deltas(1)
-    share_wait(1, 1)
-    product(1, 1)
-    scatter2(1, 0)
-    gradient(0)
+    sum_chip(1, 2)
+    sum_across(1, 2, 0)
+    sum_across(1, 2, 1)
+    product(1, 0, 0)
+    deltas(0, 1)
+    scatter_z(0, 0, 0)
+    product(1, 0, 1)
+    scatter_z(0, 0, 1)
+    scatter_y(0, 0)
+    hidden(1, 0)
+    product(0, 1, 0)
+    hidden(1, 1)
+    scatter_z(1, 0, 0)
+    product(0, 1, 1)
+    scatter_z(1, 0, 1)
+    scatter_y(1, 0)
+    deltas(1, 0)
+    product(1, 1, 0)
+    early = len(sends)
+    deltas(1, 1)
+    product(1, 1, 1)
+    scatter_z(0, 1, 0)
+    scatter_z(0, 1, 1)
+    scatter_y(0, 1)
     scattered(0, 0)
-    scatter2(0, 1)
-    gradient(1)
     scattered(1, 0)
     owners(0)
-    gradient(2)
+    gradient(0)
+    scatter_z(1, 1, 0)
+    gradient(1)
+    scatter_z(1, 1, 1)
+    scatter_y(1, 1)
     scattered(0, 1)
     send(xo_send.at[0, 1], xo_recv, xo_ss, xo_rs, peer)
-    scatter2(1, 1)
+    gradient(2)
+    sent(early)
     scattered(1, 1)
     owners(1)
     landed(xo_recv, xo_ss, xo_rs, peer)
@@ -350,8 +406,7 @@
             o_f32[:, pl.ds(at, STEP)] = t_f32[m, pl.ds(4 * k, 4), :]
     ig_ref[...] = o_f32[...].astype(BF)
 
-    for copy in sends:
-        copy.wait_send()
+    sent(len(sends))
     for store in stores:
         store.wait()
 
@@ -377,9 +432,9 @@
             pltpu.VMEM(rows, BF), pltpu.VMEM(rows, BF),
             pltpu.VMEM((4, 16, STEP), BF), pltpu.VMEM((8, 16, STEP), BF), pltpu.VMEM((XL, ROWS, TILE), F32),
             pltpu.VMEM((XL, 3, PART, CHUNK), F32), pltpu.VMEM((XL, 3, PART, CHUNK), F32), pltpu.VMEM((XL, 3, PART, CHUNK), F32),
-            pltpu.VMEM((XL, 3, PART, CHUNK), BF), pltpu.VMEM((XL, 3, PART, CHUNK), BF),
-            pltpu.VMEM((3, 2, PART, XL * CHUNK), BF), pltpu.VMEM((3, CHUNK, FFL), BF),
-            pltpu.VMEM((Z, Y, ROWS, HALF), F32), pltpu.VMEM((2,) + rows, BF),
+            pltpu.VMEM((XL, 3, 2, PART, SUB), BF), pltpu.VMEM((XL, 3, 2, PART, SUB), BF),
+            pltpu.VMEM((3, 2, PART, XL * CHUNK), BF), pltpu.VMEM((3, SUB, FFL), BF),
+            pltpu.VMEM((2, Y, ROWS, HALF), F32), pltpu.VMEM((2,) + rows, BF),
             pltpu.VMEM((2, XL, 2, 3, 4, ROWS, HALF), BF),
             pltpu.VMEM((2, XL, 2, 4, ROWS, HALF), F32), pltpu.VMEM((2, XL, 2, 4, ROWS, HALF), BF),
             pltpu.VMEM((2, XL, 2, 3, ROWS, HALF), BF),
@@ -388,8 +443,8 @@
             pltpu.VMEM((XL, 4, 16, STEP), BF), pltpu.VMEM((8, 16, STEP), BF), pltpu.VMEM((3, FFL, TILE), BF),
             sem((3,)), sem((3,)), sem((7,)), sem((7,)), sem, sem,
             sem((2, XL, 2, 3)), sem((2, XL, 2, 3)), sem((2, XL, 2, 6)), sem((2, XL, 2, 6)),
-            sem((XL, 3)), sem((XL, 3)), sem((XL, 3)), sem((XL, 3)), sem((XL, 2)), sem((XL, 2)),
-            sem((2, XL, 2, 3)), sem((2, XL, 2, 3)), sem((2, XL, 2, 3)), sem((2, XL, 2, 3)),
+            sem((XL, 3)), sem((XL, 3)), sem((XL, 3, 2)), sem((XL, 3, 2)), sem((XL, 2, 2)), sem((XL, 2, 2)),
+            sem((2, XL, 3, 3)), sem((2, XL, 3, 3)), sem((2, XL, 2, 3)), sem((2, XL, 2, 3)),
             sem, sem, sem((7,)), sem((7,)),
         ],
         compiler_params=pltpu.CompilerParams(

time: 99.5 us -> 93.4 us (0.939)
  Pallas kernels: 97.5 us -> 91.4 us
    pallas_call x1, Pallas kernels: 89.5 us -> 83.4 us  [forward_backward(): pl.pallas_call(kernel, name='ffn', out_shape=[like((ROWS, TILE), BF), lik...]
where the time goes in v3:
time: 93.4 us; the launch traced here: 92.2 us
  Pallas kernels  91.4 us (98%)
    pallas_call x1, Pallas kernels, forward_backward(): pl.pallas_call(kernel, name='ffn', out_shape=[like((ROWS, TILE), BF), lik...  83.4 us
    pallas_call x1, Pallas kernels, local(): pl.pallas_call(move, name='move', out_shape=[jax.ShapeDtypeStruct(r.shape...  8.01 us

profile of v3, /device:TPU:0, one launch (start us, length us, event | category | flops | bytes accessed | tf_op | source)
XLA Modules:
  0.0 92.2 jit_solution(3095123908931690968)
XLA Ops:
  0.6 83.4 %ffn.1 = (bf16[16,2048]{1,0:T(8,128)(2,1)}, bf16[4,8192]{1,0:T(4,128)(2,1)}, bf16[832,2048]{1,0:T(8,128)(2,1)}, bf16[832,2048]{1,0:T(8,128)(2,1)}, bf16[832,2048]{1,0:T(8,128)(2,1)}) custom-call(bf16[4,8192]{1,0:T(4,128)(2,1)} %act.1, bf16[16,2048]{1,0:T(8,128)(2,1)} %cot.1, bf16[832,2048]{1,0:T(8,128)(2,1)} %bitcast.4, bf16[832,2048]{1,0:T(8,128)(2,1)} %bitcast.5, ...), custom_call_target="tpu_custom_call" | custom-call | flops 15703474176 | bytes 20971520 | tf_op jit(solution)/shard_map/ffn/pallas_call | solution.py:421
  84.0 8.0 %move.1 = (bf16[16,2048]{1,0:T(8,128)(2,1)}, bf16[4,8192]{1,0:T(4,128)(2,1)}, bf16[832,2048]{1,0:T(8,128)(2,1)}, bf16[832,2048]{1,0:T(8,128)(2,1)}, bf16[832,2048]{1,0:T(8,128)(2,1)}) custom-call(bf16[16,2048]{1,0:T(8,128)(2,1)} %get-tuple-element.15.refs_0_, bf16[4,8192]{1,0:T(4,128)(2,1)} %get-tuple-element.16.refs_1_, ...), custom_call_target="tpu_custom_call" | custom-call | tf_op jit(solution)/shard_map/move/pallas_call | solution.py:484

commit v4 on v3

--- a/solution.py
+++ b/solution.py
@@ -31,7 +31,7 @@
 
 def kernel(
     act, cot, wg_hbm, wu_hbm, wd_hbm,
-    out_ref, ig_ref, down_hbm, gate_hbm, up_hbm,
+    out_ref, ig_ref, down_hbm, f_hbm, gd_hbm, ud_hbm,
     wg, wu, wd, feat, cota, a_send, a_recv, a_f32,
     g_send, g_own, g_recv, x_send, x_recv, hd, ht,
     part, r1_send, r1_recv, s1, r2_send, r2_recv, xo_send, xo_recv, t_f32, o_f32, n_send, n_recv, grad,
@@ -148,6 +148,17 @@
             for h in (0, 1):
                 block, there = ring_block(b, c, h, 0, part_of), ring_block_at(b, c, h, 0, part_of, d)
                 send(block, there, p2_ss.at[b, c, h, i], p2_rs.at[b, c, h, i], ring_dev(h, d))
+
+    def gather2_direct(b, c):
+        for d in (1, 2, 3):
+            for h in (0, 1):
+                block, there = ring_block(b, c, h, 0, pl.ds(0, 4)), ring_block_at(b, c, h, 0, pl.ds(0, 4), d)
+                send(block, there, p2_ss.at[b, c, h, d - 1], p2_rs.at[b, c, h, d - 1], ring_dev(h, d))
+
+    def gather2_direct_wait(b, c):
+        for d in (1, 2, 3):
+            for h in (0, 1):
+                landed(ring_block(b, c, h, d, pl.ds(0, 4)), p2_ss.at[b, c, h, d - 1], p2_rs.at[b, c, h, d - 1], ring_dev(h, d))
 
     def gather2_pass_on(b, c):
         for i, (d, part_of) in enumerate(((1, low), (3, high))):
@@ -279,16 +290,19 @@
 
     stores = []
 
-    def gradient(k):
+    def store(src, dst):
+        stores.append(pltpu.make_async_copy(src, dst, o_sem.at[len(stores)]))
+        stores[-1].start()
+
+    def down_gradient():
         def columns(j, carry):
             at = pl.ds(pl.multiple_of(j * STEP, STEP), STEP)
-            right = (cota, feat, feat)[k][:, :, :, :, at].reshape(XL * CHUNK, STEP)
-            grad[k, :, at] = dot(hd[k].reshape(FFL, XL * CHUNK), right).astype(BF)
+            right = cota[:, :, :, :, at].reshape(XL * CHUNK, STEP)
+            grad[:, at] = dot(hd[0].reshape(FFL, XL * CHUNK), right).astype(BF)
             return carry
 
         lax.fori_loop(0, TILE // STEP, columns, 0)
-        stores.append(pltpu.make_async_copy(grad.at[k], (down_hbm, gate_hbm, up_hbm)[k], o_sem.at[k]))
-        stores[-1].start()
+        store(grad, down_hbm)
 
     def sent(upto):
         for copy in sends[:upto]:
@@ -302,28 +316,23 @@
     a_recv[n] = a_send[n]
     assemble(0)
     gather1(0, 0)
+    gather1_wait(0, 0)
+    gather2_direct(0, 0)
     gather1_wait(1, 0)
     gather2(1, 0)
-    gather1_wait(0, 0)
-    gather2(0, 0)
-    gather2_pass_on(1, 0)
     assemble(1)
     gather1(0, 1)
     landed(cota.at[1, OWN, y], cx_ss, cx_rs, peer)
     gather1(1, 1)
-    gather2_pass_on(0, 0)
     for load in loads:
         load.wait()
-    gather1_wait(0, 1)
-    gather2(0, 1)
-    gather2_wait(0, 0)
+    gather2_direct_wait(0, 0)
     sum_send(0, 0)
     sum_send(0, 1)
     sum_own(0, 0)
-    gather2_wait(1, 0)
-    gather2_pass_on(0, 1)
-    gather1_wait(1, 1)
-    gather2(1, 1)
+    gather2_pass_on(1, 0)
+    gather1_wait(0, 1)
+    gather2(0, 1)
     sum_chip(0, 0)
     sum_across(0, 0, 0)
     sum_own(0, 1)
@@ -331,7 +340,11 @@
     sum_across(0, 1, 0)
     sum_across(0, 0, 1)
     sum_across(0, 1, 1)
+    gather2_wait(1, 0)
     sum_send(0, 2)
+    gather2_pass_on(0, 1)
+    gather1_wait(1, 1)
+    gather2(1, 1)
     sum_own(0, 2)
     sum_chip(0, 2)
     sum_across(0, 2, 0)
@@ -377,20 +390,21 @@
     early = len(sends)
     deltas(1, 1)
     product(1, 1, 1)
+    store(feat, f_hbm)
+    store(hd.at[1], gd_hbm)
+    store(hd.at[2], ud_hbm)
     scatter_z(0, 1, 0)
     scatter_z(0, 1, 1)
     scatter_y(0, 1)
     scattered(0, 0)
     scattered(1, 0)
     owners(0)
-    gradient(0)
+    down_gradient()
     scatter_z(1, 1, 0)
-    gradient(1)
     scatter_z(1, 1, 1)
     scatter_y(1, 1)
     scattered(0, 1)
     send(xo_send.at[0, 1], xo_recv, xo_ss, xo_rs, peer)
-    gradient(2)
     sent(early)
     scattered(1, 1)
     owners(1)
@@ -407,8 +421,8 @@
     ig_ref[...] = o_f32[...].astype(BF)
 
     sent(len(sends))
-    for store in stores:
-        store.wait()
+    for copy in stores:
+        copy.wait()
 
 
 def forward_backward(act, cot, gate_proj, up_proj, down_proj):
@@ -417,16 +431,16 @@
     sem = pltpu.SemaphoreType.DMA
     rows = (XL, Z, Y, ROWS, TILE)
     like = jax.ShapeDtypeStruct
-    flops = 2 * 9 * XL * Z * Y * ROWS * TILE * FFL
+    flops = 2 * 7 * XL * Z * Y * ROWS * TILE * FFL
     return pl.pallas_call(
         kernel,
         name="ffn",
         out_shape=[
             like((ROWS, TILE), BF), like((4, 4 * TILE), BF),
-            like((FFL, TILE), BF), like((FFL, TILE), BF), like((FFL, TILE), BF),
+            like((FFL, TILE), BF), like(rows, BF), like((2, PART, XL * CHUNK), BF), like((2, PART, XL * CHUNK), BF),
         ],
         in_specs=[vmem, vmem, any_space, any_space, any_space],
-        out_specs=[vmem, vmem] + [any_space] * 3,
+        out_specs=[vmem, vmem] + [any_space] * 4,
         scratch_shapes=[
             pltpu.VMEM((FFL, TILE), BF), pltpu.VMEM((FFL, TILE), BF), pltpu.VMEM((FFL, TILE), BF),
             pltpu.VMEM(rows, BF), pltpu.VMEM(rows, BF),
@@ -440,8 +454,8 @@
             pltpu.VMEM((2, XL, 2, 3, ROWS, HALF), BF),
             pltpu.VMEM((2, XL, ROWS, TILE), F32), pltpu.VMEM((ROWS, TILE), F32),
             pltpu.VMEM((8, 16, STEP), F32), pltpu.VMEM((4, 4 * TILE), F32),
-            pltpu.VMEM((XL, 4, 16, STEP), BF), pltpu.VMEM((8, 16, STEP), BF), pltpu.VMEM((3, FFL, TILE), BF),
-            sem((3,)), sem((3,)), sem((7,)), sem((7,)), sem, sem,
+            pltpu.VMEM((XL, 4, 16, STEP), BF), pltpu.VMEM((8, 16, STEP), BF), pltpu.VMEM((FFL, TILE), BF),
+            sem((3,)), sem((4,)), sem((7,)), sem((7,)), sem, sem,
             sem((2, XL, 2, 3)), sem((2, XL, 2, 3)), sem((2, XL, 2, 6)), sem((2, XL, 2, 6)),
             sem((XL, 3)), sem((XL, 3)), sem((XL, 3, 2)), sem((XL, 3, 2)), sem((XL, 2, 2)), sem((XL, 2, 2)),
             sem((2, XL, 3, 3)), sem((2, XL, 3, 3)), sem((2, XL, 2, 3)), sem((2, XL, 2, 3)),
@@ -454,43 +468,69 @@
     )(act, cot, gate_proj, up_proj, down_proj)
 
 
-SLABS = 4
-
-
-def move(*refs):
-    srcs, dsts, held, sem_in, sem_out = refs[:5], refs[5:10], refs[10:15], refs[15], refs[16]
-    parts = []
-    for src, via, dst in zip(srcs, held, dsts):
-        slabs = SLABS if src.shape[0] == FFL else 1
-        rows = src.shape[0] // slabs
-        for i in range(slabs):
-            at, j = pl.ds(i * rows, rows), len(parts)
-            parts.append((
-                pltpu.make_async_copy(src.at[at], via.at[at], sem_in.at[j]),
-                pltpu.make_async_copy(via.at[at], dst.at[at], sem_out.at[j]),
-            ))
-    for load, _ in parts:
+def finish(
+    out, ig, down, feat, gate_delta, up_delta, out_to, ig_to, down_to, gate_to, up_to,
+    out_v, ig_v, down_v, feat_v, gd_v, ud_v, gate_v, up_v, sem_in, sem_out,
+):
+    blocks = TILE // STEP
+    cols = [pl.ds(j * STEP, STEP) for j in range(blocks)]
+    load_gd = pltpu.make_async_copy(gate_delta, gd_v, sem_in.at[0])
+    load_ud = pltpu.make_async_copy(up_delta, ud_v, sem_in.at[1])
+    load_feat = [pltpu.make_async_copy(feat.at[:, at], feat_v.at[:, at], sem_in.at[2 + j]) for j, at in enumerate(cols)]
+    passed = ((down, down_v, down_to), (out, out_v, out_to), (ig, ig_v, ig_to))
+    load_rest = [pltpu.make_async_copy(src, via, sem_in.at[2 + blocks + i]) for i, (src, via, _) in enumerate(passed)]
+    load_gd.start()
+    for load in load_feat:
         load.start()
-    for load, store in parts:
+    load_ud.start()
+    for load in load_rest:
+        load.start()
+    stores = []
+
+    def store(src, dst):
+        stores.append(pltpu.make_async_copy(src, dst, sem_out.at[len(stores)]))
+        stores[-1].start()
+
+    load_gd.wait()
+    for j, at in enumerate(cols):
+        load_feat[j].wait()
+        gate_v[:, at] = dot(gd_v[...], feat_v[:, at]).astype(BF)
+        store(gate_v.at[:, at], gate_to.at[:, at])
+    load_ud.wait()
+    for load, (_, via, dst) in zip(load_rest, passed):
         load.wait()
-        store.start()
-    for _, store in parts:
-        store.wait()
+        store(via, dst)
+    for at in cols:
+        up_v[:, at] = dot(ud_v[...], feat_v[:, at]).astype(BF)
+        store(up_v.at[:, at], up_to.at[:, at])
+    for copy in stores:
+        copy.wait()
 
 
 def local(activations, cotangent, gate_proj, up_proj, down_proj):
-    results = forward_backward(activations, cotangent, gate_proj.T, up_proj.T, down_proj)
+    block_output, input_gradient, down_gradient, features, gate_delta, up_delta = forward_backward(
+        activations, cotangent, gate_proj.T, up_proj.T, down_proj
+    )
     any_space = pl.BlockSpec(memory_space=pl.ANY)
+    like = jax.ShapeDtypeStruct
+    width = XL * CHUNK
     block_output, input_gradient, down_gradient, gate_gradient, up_gradient = pl.pallas_call(
-        move,
-        name="move",
-        out_shape=[jax.ShapeDtypeStruct(r.shape, r.dtype) for r in results],
-        in_specs=[any_space] * 5,
+        finish,
+        name="finish",
+        out_shape=[like((ROWS, TILE), BF), like((4, 4 * TILE), BF)] + [like((FFL, TILE), BF)] * 3,
+        in_specs=[any_space] * 6,
         out_specs=[any_space] * 5,
-        scratch_shapes=[pltpu.VMEM(r.shape, r.dtype) for r in results]
-        + [pltpu.SemaphoreType.DMA((3 * SLABS + 2,))] * 2,
+        scratch_shapes=[
+            pltpu.VMEM((ROWS, TILE), BF), pltpu.VMEM((4, 4 * TILE), BF), pltpu.VMEM((FFL, TILE), BF),
+            pltpu.VMEM((width, TILE), BF), pltpu.VMEM((FFL, width), BF), pltpu.VMEM((FFL, width), BF),
+            pltpu.VMEM((FFL, TILE), BF), pltpu.VMEM((FFL, TILE), BF),
+            pltpu.SemaphoreType.DMA((9,)), pltpu.SemaphoreType.DMA((11,)),
+        ],
         compiler_params=pltpu.CompilerParams(vmem_limit_bytes=62 * 1024 * 1024),
-    )(*results)
+    )(
+        block_output, input_gradient, down_gradient, features.reshape(width, TILE),
+        gate_delta.reshape(FFL, width), up_delta.reshape(FFL, width),
+    )
     return block_output, input_gradient, gate_gradient.T, up_gradient.T, down_gradient
 
 

time: 93.4 us -> 92.2 us (0.987)
  Pallas kernels: 91.4 us -> 90.2 us
    pallas_call x1, Pallas kernels: 8.01 us -> 7.01 us  [local(): pl.pallas_call(finish, name='finish', out_shape=[like((ROWS, TILE), BF),...]
where the time goes in v4:
time: 92.2 us; the launch traced here: 91 us
  Pallas kernels  90.2 us (98%)
    pallas_call x1, Pallas kernels, forward_backward(): pl.pallas_call(kernel, name='ffn', out_shape=[like((ROWS, TILE), BF), lik...  83.2 us
    pallas_call x1, Pallas kernels, local(): pl.pallas_call(finish, name='finish', out_shape=[like((ROWS, TILE), BF),...  7.01 us

profile of v4, /device:TPU:0, one launch (start us, length us, event | category | flops | bytes accessed | tf_op | source)
XLA Modules:
  0.0 91.0 jit_solution(16803278510491671085)
XLA Ops:
  0.6 83.2 %ffn.1 = (bf16[16,2048]{1,0:T(8,128)(2,1)}, bf16[4,8192]{1,0:T(4,128)(2,1)}, bf16[832,2048]{1,0:T(8,128)(2,1)}, bf16[2,4,4,16,2048]{4,3,2,1,0:T(8,128)(2,1)}, bf...) custom-call(bf16[4,8192]{1,0:T(4,128)(2,1)} %act.1, bf16[16,2048]{1,0:T(8,128)(2,1)} %cot.1, ...), custom_call_target="tpu_custom_call" | custom-call | flops 12213813248 | bytes 20971520 | tf_op jit(solution)/shard_map/ffn/pallas_call | solution.py:435
  83.9 7.0 %finish.1 = (bf16[16,2048]{1,0:T(8,128)(2,1)}, bf16[4,8192]{1,0:T(4,128)(2,1)}, bf16[832,2048]{1,0:T(8,128)(2,1)}, bf16[832,2048]{1,0:T(8,128)(2,1)}, bf16[832,2048]{1,0:T(8,128)(2,1)}) custom-call(bf16[16,2048]{1,0:T(8,128)(2,1)} %get-tuple-element.16.out, bf16[4,8192]{1,0:T(4,128)(2,1)} %get-tuple-element.17.ig, bf16[832,2048]{1,0:T(8,128)(2,1)} %get-tuple-element.18.down, ...), custom_call_target="tpu_custom_call" | custom-call | tf_op jit(solution)/shard_map/finish/pallas_call | solution.py:517

commit v5 on v4

--- a/solution.py
+++ b/solution.py
@@ -399,12 +399,12 @@
     scattered(0, 0)
     scattered(1, 0)
     owners(0)
-    down_gradient()
     scatter_z(1, 1, 0)
     scatter_z(1, 1, 1)
     scatter_y(1, 1)
     scattered(0, 1)
     send(xo_send.at[0, 1], xo_recv, xo_ss, xo_rs, peer)
+    down_gradient()
     sent(early)
     scattered(1, 1)
     owners(1)

time: 92.2 us -> 92.2 us (level)
  no operation moved by 1% of the time
where the time goes in v5:
time: 92.2 us; the launch traced here: 91 us
  Pallas kernels  90.2 us (98%)
    pallas_call x1, Pallas kernels, forward_backward(): pl.pallas_call(kernel, name='ffn', out_shape=[like((ROWS, TILE), BF), lik...  83.2 us
    pallas_call x1, Pallas kernels, local(): pl.pallas_call(finish, name='finish', out_shape=[like((ROWS, TILE), BF),...  7.01 us

profile of v5, /device:TPU:0, one launch (start us, length us, event | category | flops | bytes accessed | tf_op | source)
XLA Modules:
  0.0 91.0 jit_solution(1980013213849208119)
XLA Ops:
  0.6 83.2 %ffn.1 = (bf16[16,2048]{1,0:T(8,128)(2,1)}, bf16[4,8192]{1,0:T(4,128)(2,1)}, bf16[832,2048]{1,0:T(8,128)(2,1)}, bf16[2,4,4,16,2048]{4,3,2,1,0:T(8,128)(2,1)}, bf...) custom-call(bf16[4,8192]{1,0:T(4,128)(2,1)} %act.1, bf16[16,2048]{1,0:T(8,128)(2,1)} %cot.1, ...), custom_call_target="tpu_custom_call" | custom-call | flops 12213813248 | bytes 20971520 | tf_op jit(solution)/shard_map/ffn/pallas_call | solution.py:435
  83.9 7.0 %finish.1 = (bf16[16,2048]{1,0:T(8,128)(2,1)}, bf16[4,8192]{1,0:T(4,128)(2,1)}, bf16[832,2048]{1,0:T(8,128)(2,1)}, bf16[832,2048]{1,0:T(8,128)(2,1)}, bf16[832,2048]{1,0:T(8,128)(2,1)}) custom-call(bf16[16,2048]{1,0:T(8,128)(2,1)} %get-tuple-element.16.out, bf16[4,8192]{1,0:T(4,128)(2,1)} %get-tuple-element.17.ig, bf16[832,2048]{1,0:T(8,128)(2,1)} %get-tuple-element.18.down, ...), custom_call_target="tpu_custom_call" | custom-call | tf_op jit(solution)/shard_map/finish/pallas_call | solution.py:517
